TPU v7x, 256 devices: a whole 4x4x8 slice. The times are simulated.
256 devices in a mesh: samp: 32 (over x, z), prot: 8 (over y, core).
Axes of the slice: x: 4, y: 4, z: 8, core: 2. Of those that a mesh axis runs over, the one named last changes fastest.
Arguments:
- bin_ids: int32 [736, 131072], P('prot', 'samp'), may hold values from 0 to 1023
- plate_ids: int32 [131072], P('samp'), may hold values from 0 to 23, as said below
- covariates: float32 [40, 131072], P(None, 'samp'), may hold values from -50 to 50
- dosages: bfloat16 [1024, 131072], P(None, 'samp'), may hold values from 0 to 2
Outputs:
- t_stats: float32 [1024, 736], P('samp', 'prot')
Inputs may be any that keep to these rules, and one draw needn't show every extreme that they name: `plate_ids`: every plate holds at least one sample.
All inputs are finite; a program needn't handle non-finite values.
Results may differ from a plain program's by a relative error of at most 0.0003.
Values sent between devices are 32-bit elements; how exact they have to be, the bound alone decides.
No kernel may reach another device: no remote copies, remote signals or barrier semaphores. Data moves between devices by JAX's collectives and lax.ppermute only.
A program may use at most 128 MiB of HBM per device.

v0:
```python
import math

import jax
import jax.numpy as jnp
from jax import lax
from jax.sharding import PartitionSpec as P

BINS = 1024
BIN_LOW = 32
PLATES = 24
DESIGN = 64


exact_mode = lax.Precision.HIGHEST
tiny_eps = 1e-06


def normal_quantile(level):
    return math.sqrt(2.0) * lax.erf_inv(2.0 * level - 1.0)


def block_width(sample_width):
    return math.gcd(sample_width, 512)


def local_counts(bin_ids):
    high_count = BINS // BIN_LOW
    sample_width = bin_ids.shape[1]
    block_size = block_width(sample_width)
    high_ids = jnp.arange(high_count, dtype=jnp.int32)[None, :, None]
    low_ids = jnp.arange(BIN_LOW, dtype=jnp.int32)[None, :, None]

    def add_block(running, counter):
        segment = lax.dynamic_slice_in_dim(bin_ids, counter * block_size, block_size, 1)[:, None, :]
        upper_hot = (segment // BIN_LOW == high_ids).astype(jnp.bfloat16)
        lower_hot = (segment % BIN_LOW == low_ids).astype(jnp.bfloat16)
        return (
            running
            + jnp.einsum("pas,pbs->pab", upper_hot, lower_hot, preferred_element_type=jnp.float32),
            None,
        )

    start_value = jnp.zeros((bin_ids.shape[0], high_count, BIN_LOW), jnp.float32)
    running, _ = lax.scan(add_block, start_value, jnp.arange(sample_width // block_size))
    return running.reshape(bin_ids.shape[0], BINS)


def rank_table(counts, sample_total):
    lower_index = jnp.arange(BINS, dtype=jnp.int32)[:, None]
    upper_index = jnp.arange(BINS, dtype=jnp.int32)[None, :]
    strict_upper = (lower_index < upper_index).astype(jnp.float32)
    preceding = jnp.dot(
        counts, strict_upper, precision=exact_mode, preferred_element_type=jnp.float32
    )
    middle = preceding + 0.5 * (counts + 1.0)
    return normal_quantile((middle - 0.375) / (sample_total + 0.25))


def lookup_levels(rank_values, bin_ids):
    high_count = BINS // BIN_LOW
    row_total = bin_ids.shape[0]
    sample_width = bin_ids.shape[1]
    block_size = block_width(sample_width)
    block_total = sample_width // block_size
    table = rank_values.reshape(row_total, high_count, BIN_LOW)
    high_ids = jnp.arange(high_count, dtype=jnp.int32)[None, :, None]
    low_ids = jnp.arange(BIN_LOW, dtype=jnp.int32)[None, :, None]

    def one_block(counter):
        segment = lax.dynamic_slice_in_dim(bin_ids, counter * block_size, block_size, 1)[:, None, :]
        lower_hot = (segment % BIN_LOW == low_ids).astype(jnp.float32)
        picked = jnp.einsum(
            "pab,pbs->pas",
            table,
            lower_hot,
            precision=exact_mode,
            preferred_element_type=jnp.float32,
        )
        upper_mask = segment // BIN_LOW == high_ids
        return jnp.sum(jnp.where(upper_mask, picked, 0.0), axis=1)

    blocks = lax.map(one_block, jnp.arange(block_total))
    return jnp.transpose(blocks, (1, 0, 2)).reshape(row_total, sample_width)


def build_design(covariates, plate_ids):
    plate_rows = (plate_ids[None, :] == jnp.arange(PLATES, dtype=jnp.int32)[:, None]).astype(
        jnp.float32
    )
    return jnp.concatenate([covariates, plate_rows], axis=0)


def design_terms(design, dosages):
    gram_part = jnp.einsum(
        "ks,js->kj", design, design, precision=exact_mode, preferred_element_type=jnp.float32
    )
    dose_cross = jnp.einsum(
        "ks,vs->kv", design, dosages, precision=exact_mode, preferred_element_type=jnp.float32
    )
    dose_float = dosages.astype(jnp.float32)
    dose_square = jnp.sum(dose_float * dose_float, axis=1)
    return (gram_part, dose_cross, dose_square)


def body(bin_ids, plate_ids, covariates, dosages):
    sample_width = bin_ids.shape[1]
    sample_total = sample_width * lax.axis_size("samp")
    design = build_design(covariates, plate_ids)
    local_hist = local_counts(bin_ids)
    share_size = sample_width // lax.axis_size("prot")
    begin_at = lax.axis_index("prot") * share_size
    design_part = lax.dynamic_slice_in_dim(design, begin_at, share_size, 1)
    dose_part = lax.dynamic_slice_in_dim(dosages, begin_at, share_size, 1)
    gram_part, dose_cross, dose_square = design_terms(design_part, dose_part)
    gram_sum, dose_proj, dose_sq = lax.psum((gram_part, dose_cross, dose_square), ("samp", "prot"))
    counts = lax.psum(local_hist, "samp")
    rank_values = rank_table(counts, sample_total)
    expressed = lookup_levels(rank_values, bin_ids)
    chol_factor = jnp.linalg.cholesky(gram_sum)
    dose_load = jax.scipy.linalg.cho_solve((chol_factor, True), dose_proj)
    expr_cross = jnp.einsum(
        "ks,ps->kp", design, expressed, precision=exact_mode, preferred_element_type=jnp.float32
    )
    expr_square = jnp.sum(expressed * expressed, axis=1)
    expr_proj, expr_sq = lax.psum((expr_cross, expr_square), "samp")
    prot_load = jax.scipy.linalg.cho_solve((chol_factor, True), expr_proj)
    dose_norm = dose_sq - jnp.sum(dose_proj * dose_load, axis=0)
    expr_norm = expr_sq - jnp.sum(expr_proj * prot_load, axis=0)
    row_count = dosages.shape[0] // lax.axis_size("samp")
    own_start = lax.axis_index("samp") * row_count
    dose_resid = dosages - jnp.einsum(
        "kv,ks->vs", dose_load, design, precision=exact_mode, preferred_element_type=jnp.float32
    )
    expr_resid = expressed - jnp.einsum(
        "kp,ks->ps", prot_load, design, precision=exact_mode, preferred_element_type=jnp.float32
    )
    cross = lax.psum_scatter(
        jnp.einsum(
            "vs,ps->vp",
            dose_resid,
            expr_resid,
            precision=exact_mode,
            preferred_element_type=jnp.float32,
        ),
        "samp",
        scatter_dimension=0,
        tiled=True,
    )
    dose_rows = lax.dynamic_slice_in_dim(dose_norm, own_start, row_count, 0)
    corr = cross * lax.rsqrt(dose_rows[:, None] * expr_norm[None, :] + tiny_eps)
    freedom = sample_total - DESIGN - 1.0
    return corr * jnp.sqrt(freedom / (1.0 - corr * corr))


def solution(mesh):
    placed = (P("prot", "samp"), P("samp"), P(None, "samp"), P(None, "samp"))
    return jax.shard_map(
        body, mesh=mesh, in_specs=placed, out_specs=P("samp", "prot"), check_vma=False
    )
```

profile of v0, /device:TPU:26, one launch (start us, length us, event | category | flops | bytes accessed | tf_op | source)
XLA Modules:
  0.0 860.3 jit_solution(17107157144385160508)
XLA Ops:
  7.4 3.1 fusion.22
  10.6 28.4 %while.31 = (s32[]{:T(128)}, f32[92,32,32]{2,1,0:T(8,128)S(1)}, s32[8]{0:T(128)S(1)}, s32[92,4096]{1,0:T(8,128)S(1)}, s32[]{:T(128)}, /*index=5*/s32[1]{0:T(128)}, s32[]{:T(128)}, s32[]{:T(128)}) while((s32[]{:T(128)}, f32[92,32,32]{2,1,0:T(8,128)S(1)}, s32[8]{0:T(128)S(1)}, s32[92,4096]{1,0:T(8,128)S(1)}, s32[]{:T(128)}, ...), condition=%wide.region_5.6_spmd.clone.clone, body=%wide.region_4.5_spmd.clone.clone.sunk | while | flops 100849672 | bytes 1978537 | solution.py:44
  12.2 1.9 select_add_fusion.2
  15.7 1.9 select_add_fusion.2
  19.3 1.9 select_add_fusion.2
  22.8 1.9 select_add_fusion.2
  26.4 1.9 select_add_fusion.2
  29.9 1.9 select_add_fusion.2
  33.5 1.9 select_add_fusion.2
  37.0 1.9 select_add_fusion.2
  40.1 2.2 copy.9
  45.2 78.5 %all-reduce = (f32[64,64]{0,1:T(8,128)S(1)}, f32[1024]{0:T(1024)S(1)}) all-reduce(f32[64,64]{0,1:T(8,128)S(1)} %fusion.46, f32[1024]{0:T(1024)S(1)} %multiply_reduce_fusion), channel_id=1, replica_groups=mesh['samp'=32,'prot'=8] {'samp','prot'}, use_global_device_ids=true, to_apply=%region_0.1 | all-reduce | flops 5120 | bytes 40960 | tf_op jit(solution)/shard_map/psum | solution.py:115
  123.8 5.8 cholesky.16
  131.1 4.9 custom-call.16
  136.0 129.5 %all-reduce.5.cloned.1.call-done = f32[64,1024]{1,0:T(8,128)} async-done(((f32[64,1024]{1,0:T(8,128)}), f32[64,1024]{1,0:T(8,128)}) %all-reduce.5.cloned.1.call-update) | async-done | bytes 262160 | tf_op jit(solution)/shard_map/psum | solution.py:115
  268.2 16.0 %fusion.25 = f32[1024,4096]{1,0:T(8,128)} fusion(f32[64,1024]{1,0:T(8,128)S(1)} %get-tuple-element.288, f32[24,4096]{1,0:T(8,128)S(1)} %fusion.29, f32[40,4096]{1,0:T(8,128)S(1)} %copy-done), kind=kOutput, calls=%fused_computation.51 | convolution fusion | flops 3221487616 | bytes 18087936 | tf_op jit(solution)/shard_map/kv,ks->vs/dot_general | solution.py:131
  284.2 128.0 %all-reduce.7.cloned.1.call-done = f32[92,1024]{1,0:T(8,128)} async-done(((f32[92,1024]{1,0:T(8,128)}), f32[92,1024]{1,0:T(8,128)}) %all-reduce.7.cloned.1.call-update) | async-done | bytes 376848 | tf_op jit(solution)/shard_map/psum | solution.py:116
  412.2 3.4 select_multiply_fusion
  416.8 2.2 copy.12
  419.0 59.8 %while.30 = (s32[]{:T(128)}, f32[8,92,512]{2,1,0:T(8,128)}, s32[8]{0:T(128)S(1)}, s32[92,4096]{1,0:T(8,128)S(1)}, f32[92,32,32]{2,1,0:T(8,128)}, /*index=5*/s32[]{:T(128)}, s32[1]{0:T(128)}, s32[]{:T(128)}, s32[]{:T(128)}) while((s32[]{:T(128)}, f32[8,92,512]{2,1,0:T(8,128)}, s32[8]{0:T(128)S(1)}, ...), condition=%wide.region_9.10_spmd.clone.clone, body=%wide.region_7.9_spmd.clone.clone.sunk | while | flops 585973760 | bytes 2175147 | solution.py:82
  420.5 5.3 fusion.61
  428.0 5.3 fusion.61
  435.5 5.3 fusion.61
  442.9 5.3 fusion.61
  450.4 5.3 fusion.61
  457.9 5.3 fusion.61
  465.3 5.3 fusion.61
  472.8 5.3 fusion.61
  478.8 1.8 multiply_reduce_fusion.1
  484.5 129.8 %all-reduce.1 = (f32[64,92]{1,0:T(8,128)S(1)}, f32[92]{0:T(128)S(1)}) all-reduce(f32[64,92]{1,0:T(8,128)S(1)} %fusion.24, f32[92]{0:T(128)S(1)} %multiply_reduce_fusion.1), channel_id=1, replica_groups=mesh['samp'=32,'prot'=8] {'samp'}, use_global_device_ids=true, to_apply=%region_10.11 | all-reduce | flops 5980 | bytes 47840 | tf_op jit(solution)/shard_map/psum | solution.py:125
  616.3 17.9 %fusion.14 = f32[1024,92]{1,0:T(8,128)} fusion(f32[92,4096]{1,0:T(8,128)S(1)} %convolution_subtract_fusion, f32[1024,4096]{1,0:T(8,128)} %fusion.25, bf16[1024,4096]{1,0:T(8,128)(2,1)} %param.11), kind=kOutput, calls=%fused_computation.33 | convolution fusion | flops 4638900224 | bytes 27049984 | tf_op jit(solution)/shard_map/vs,ps->vp/dot_general | solution.py:138
  634.3 218.0 %reduce-scatter.2.cloned.1.call-done = f32[32,92]{1,0:T(8,128)} async-done(((f32[1024,92]{1,0:T(8,128)}), f32[32,92]{1,0:T(8,128)}) %reduce-scatter.2.cloned.1.call-update) | async-done | bytes 11792 | tf_op jit(solution)/shard_map/reduce_scatter | solution.py:137
  (97 shorter events, 37.0 us)
Async XLA Ops:
  6.5 4.0 copy-start.1
  6.5 259.0 %all-reduce.5.cloned.1.call-start = ((), (), s32[]{:S(2)}) async-start(), calls=%async_computation.1 | async-start | bytes 524288 | tf_op jit(solution)/shard_map/psum | solution.py:115
  10.5 401.7 %all-reduce.7.cloned.1.call-start = ((), (), s32[]{:S(2)}) async-start(), calls=%async_computation.2 | async-start | bytes 786432 | tf_op jit(solution)/shard_map/psum | solution.py:116
  38.9 1.2 copy-start.3
  42.3 2.6 copy-start
  43.3 809.0 %reduce-scatter.2.cloned.1.call-start = ((), (), s32[]{:S(2)}) async-start(), calls=%async_computation.3 | async-start | bytes 540672 | tf_op jit(solution)/shard_map/reduce_scatter | solution.py:137
  478.8 1.9 copy-start.2
Sparse Core Ops, SparseCore 0:
  12.8 252.6 all-reduce.4
  268.9 143.2 all-reduce.6
  634.3 217.9 reduce-scatter.1
where the time goes:
time: 862 us; the launch traced here: 860 us
  waiting for transfers between devices  476 us (55%)
  blocking collectives  208 us (24%)
  matrix products  105 us (12%)
  local copies, waits for them, and re-layouts  25.8 us (3%)
  other arithmetic  21.4 us (2%)
  between operations  13.3 us (2%)
  loops' own time  11.2 us (1%)
    reduce_scatter x1, waiting for transfers between devices, body(): lax.psum_scatter(jnp.einsum('vs,ps->vp', dose_resid, expr_resid, precisio...  218 us
    psum x1, blocking collectives, body(): expr_proj, expr_sq = lax.psum((expr_cross, expr_square), 'samp')  130 us
    psum x1, waiting for transfers between devices, body(): lax.psum((gram_part, dose_cross, dose_square), ('samp', 'prot'))  130 us
    psum x1, waiting for transfers between devices, body(): counts = lax.psum(local_hist, 'samp')  128 us
    psum x1, blocking collectives, body(): lax.psum((gram_part, dose_cross, dose_square), ('samp', 'prot'))  78.5 us
    dot_general x8, matrix products, one_block(): jnp.einsum('pab,pbs->pas', table, lower_hot, precision=exact_mode, prefer...  42.2 us
    dot_general x1, matrix products, body(): jnp.einsum('vs,ps->vp', dose_resid, expr_resid, precision=exact_mode, pre...  17.9 us
  transfers between devices with their start and end apart: 3, of which 3 were waited for; matrix products, arithmetic and copies ran while one was open for 7% of the time, Pallas kernels for 0%

commit v1 on v0

v1 whole, which is shorter than its diff:
```python
import functools
import math

import jax
import jax.numpy as jnp
from jax import lax
from jax.experimental import pallas as pl
from jax.experimental.pallas import tpu as pltpu
from jax.sharding import PartitionSpec as P

BINS = 1024
PLATES = 24
COVARS = 40
DESIGN = 64
LANES = 128
tiny_eps = 1e-06
F32 = jnp.float32
BF16 = jnp.bfloat16
exact_mode = lax.Precision.HIGHEST
NT = (((1,), (1,)), ((), ()))
NN = (((1,), (0,)), ((), ()))


def vmem_params(mib):
    return pltpu.CompilerParams(vmem_limit_bytes=mib * 1024 * 1024)


def lane_ids(shape):
    return lax.broadcasted_iota(jnp.int32, shape, len(shape) - 1)


def design_parts(cov, plates):
    width = cov.shape[1]
    rows = lax.broadcasted_iota(jnp.int32, (PLATES, width), 0)
    plate_rows = jnp.where(plates == rows, 1.0, 0.0).astype(F32)
    design = jnp.concatenate([cov, plate_rows], axis=0)
    high = design.astype(BF16)
    rest = design - high.astype(F32)
    middle = rest.astype(BF16)
    low = (rest - middle.astype(F32)).astype(BF16)
    return high, middle, low


def fold_lanes(wide):
    first, second = wide[:, :LANES], wide[:, LANES:]
    pair = first + second
    return pair + pltpu.roll(pair, 64, 1)


def hist_kernel(bins_ref, cov_ref, plate_ref, out_ref, table_ref):
    step = pl.program_id(0)
    width = bins_ref.shape[1]
    chunk = 1024
    ids32 = lax.broadcasted_iota(jnp.int32, (32, chunk), 0)
    total = jnp.zeros((256, 256), F32)
    for start in range(0, width, chunk):
        bins = bins_ref[:, start : start + chunk]
        upper, lower = bins >> 5, bins & 31
        left = jnp.concatenate(
            [jnp.where(upper[p : p + 1] == ids32, 1.0, 0.0).astype(BF16) for p in range(8)], axis=0
        )
        right = jnp.concatenate(
            [jnp.where(lower[p : p + 1] == ids32, 1.0, 0.0).astype(BF16) for p in range(8)], axis=0
        )
        total = total + lax.dot_general(left, right, NT, preferred_element_type=F32)
    lane = lane_ids((32, 256)) // 32
    diag = jnp.zeros((32, 256), F32)
    for p in range(8):
        diag = jnp.where(lane == p, total[32 * p : 32 * p + 32], diag)
    table_ref[...] = diag[:, :LANES]
    table_ref2 = table_ref
    block = lane_ids((8, LANES)) // 32
    for half in range(2):
        table_ref2[...] = diag[:, half * LANES : (half + 1) * LANES]
        rows = [table_ref2[pl.ds(c, 8, stride=4), :] for c in range(4)]
        for q in range(4):
            out = jnp.zeros((8, LANES), F32)
            for c in range(4):
                shift = ((c - q) % 4) * 32
                moved = pltpu.roll(rows[c], shift, 1) if shift else rows[c]
                out = jnp.where(block == c, moved, out)
            p = half * 4 + q
            out_ref[8 * p : 8 * p + 8, :] = out

    @pl.when(step == pl.num_programs(0) - 1)
    def _():
        high, middle, low = design_parts(cov_ref[...], plate_ref[...])
        stack = jnp.concatenate([high, middle, low, jnp.zeros_like(high)], axis=0)
        wide = lax.dot_general(stack[:192], stack, NT, preferred_element_type=F32)
        gram = fold_lanes(wide[:64] + wide[64:128] + wide[128:192])
        out_ref[32:64, :] = jnp.where(lane_ids((32, LANES)) < 64, gram[:32], gram[32:])


def histogram(bin_ids, covariates, plates):
    width = bin_ids.shape[1]
    return pl.pallas_call(
        hist_kernel,
        grid=(12,),
        in_specs=[
            pl.BlockSpec((8, width), lambda g: (g, 0)),
            pl.BlockSpec((COVARS, width), lambda g: (0, 0)),
            pl.BlockSpec((1, width), lambda g: (0, 0)),
        ],
        out_specs=pl.BlockSpec((64, LANES), lambda g: (g, 0)),
        out_shape=jax.ShapeDtypeStruct((768, LANES), F32),
        scratch_shapes=[pltpu.VMEM((32, LANES), F32)],
        compiler_params=vmem_params(48),
        name="histogram",
    )(bin_ids, covariates, plates)


def dose_kernel(dose_ref, cov_ref, plate_ref, proj_ref, square_ref, total_ref):
    step = pl.program_id(0)
    high, middle, low = design_parts(cov_ref[...], plate_ref[...])
    stack = jnp.concatenate([high, middle, low, jnp.zeros_like(high)], axis=0)
    dose = dose_ref[...]
    term = lax.dot_general(dose, stack, NT, preferred_element_type=F32)
    wide = dose.astype(F32)
    wide = wide * wide
    part = wide[:, :LANES]
    for start in range(LANES, wide.shape[1], LANES):
        part = part + wide[:, start : start + LANES]

    @pl.when(step == 0)
    def _():
        total_ref[...] = term
        square_ref[...] = part

    @pl.when(step > 0)
    def _():
        total_ref[...] += term
        square_ref[...] += part

    @pl.when(step == pl.num_programs(0) - 1)
    def _():
        half = lane_ids((16, LANES)) < 64
        for c in range(32):
            both = fold_lanes(total_ref[32 * c : 32 * c + 32, :])
            proj_ref[16 * c : 16 * c + 16, :] = jnp.where(half, both[:16], both[16:])


def dose_products(dosages, covariates, plates):
    count, width = dosages.shape
    tile = 512
    return pl.pallas_call(
        dose_kernel,
        grid=(width // tile,),
        in_specs=[
            pl.BlockSpec((count, tile), lambda s: (0, s)),
            pl.BlockSpec((COVARS, tile), lambda s: (0, s)),
            pl.BlockSpec((1, tile), lambda s: (0, s)),
        ],
        out_specs=[
            pl.BlockSpec((count // 2, LANES), lambda s: (0, 0)),
            pl.BlockSpec((count, LANES), lambda s: (0, 0)),
        ],
        out_shape=[
            jax.ShapeDtypeStruct((count // 2, LANES), F32),
            jax.ShapeDtypeStruct((count, LANES), F32),
        ],
        scratch_shapes=[pltpu.VMEM((count, 256), F32)],
        compiler_params=vmem_params(32),
        cost_estimate=pl.CostEstimate(
            flops=2 * count * width * 256, bytes_accessed=count * width * 2, transcendentals=0
        ),
        name="dose_products",
    )(dosages, covariates, plates)


def erf_inverse(x):
    w = -jnp.log1p(-x * x)
    small = w < 5.0
    shifted = jnp.where(small, w - 2.5, jnp.sqrt(w) - 3.0)
    near = (
        2.81022636e-08, 3.43273939e-07, -3.5233877e-06, -4.39150654e-06, 0.00021858087,
        -0.00125372503, -0.00417768164, 0.246640727, 1.50140941,
    )
    far = (
        -0.000200214257, 0.000100950558, 0.00134934322, -0.00367342844, 0.00573950773,
        -0.0076224613, 0.00943887047, 1.00167406, 2.83297682,
    )
    value = jnp.where(small, near[0], far[0])
    for a, b in zip(near[1:], far[1:]):
        value = value * shifted + jnp.where(small, a, b)
    return value * x


def table_kernel(sample_total, base_ref, parts_ref, out_ref):
    counts = jnp.sum(parts_ref[...], axis=0)
    rows = counts.shape[0]
    row = lax.broadcasted_iota(jnp.int32, (LANES, LANES), 0)
    before = (row < lane_ids((LANES, LANES))).astype(F32)
    inside = lax.dot_general(
        counts, before, NN, precision=exact_mode, preferred_element_type=F32
    )
    totals = jnp.broadcast_to(jnp.sum(counts, axis=1, keepdims=True), counts.shape)
    row = lax.broadcasted_iota(jnp.int32, (rows, rows), 0)
    col = lane_ids((rows, rows))
    earlier = ((col < row) & (col // 8 == row // 8)).astype(F32)
    outside = lax.dot_general(
        earlier, totals, NN, precision=exact_mode, preferred_element_type=F32
    )
    middle = inside + outside + 0.5 * (counts + 1.0)
    level = (middle - 0.375) / (sample_total + 0.25)
    values = math.sqrt(2.0) * erf_inverse(2.0 * level - 1.0)
    place = base_ref[0] + lax.broadcasted_iota(jnp.int32, counts.shape, 0)
    values = jnp.where(place < 736, values, counts)
    for n in range(out_ref.shape[0]):
        out_ref[n] = values


def rank_table(parts, sample_total, base):
    return pl.pallas_call(
        functools.partial(table_kernel, float(sample_total)),
        in_specs=[
            pl.BlockSpec(memory_space=pltpu.SMEM),
            pl.BlockSpec(memory_space=pltpu.VMEM),
        ],
        out_specs=pl.BlockSpec(memory_space=pltpu.VMEM),
        out_shape=jax.ShapeDtypeStruct(parts.shape, F32),
        compiler_params=vmem_params(16),
        name="rank_table",
    )(base, parts)


def cross_kernel(
    bins_ref, table_ref, dose_ref, cov_ref, plate_ref, dproj_ref, dsq_ref,
    out_ref, level_ref, total_ref, design_ref, square_ref,
):
    step = pl.program_id(0)
    tile = bins_ref.shape[1]

    @pl.when(step == 0)
    def _():
        level_ref[...] = jnp.zeros_like(level_ref)
        total_ref[...] = jnp.zeros_like(total_ref)
        design_ref[...] = jnp.zeros_like(design_ref)
        square_ref[...] = jnp.zeros_like(square_ref)

    for g in range(0, 12, 2):
        highs, lows = [[], []], [[], []]
        for half in range(2):
            first = g + half
            tables = [table_ref[pl.ds(64 * first + k, 8, stride=8), :] for k in range(8)]
            pieces = []
            for start in range(0, tile, LANES):
                bins = bins_ref[8 * first : 8 * first + 8, start : start + LANES]
                lower, upper = bins & 127, bins >> 7
                value = jnp.take_along_axis(tables[0], lower, axis=1, mode="promise_in_bounds")
                for k in range(1, 8):
                    other = jnp.take_along_axis(tables[k], lower, axis=1, mode="promise_in_bounds")
                    value = jnp.where(upper == k, other, value)
                if first == 11:
                    keep = lax.broadcasted_iota(jnp.int32, (8, LANES), 0) < 4
                    value = jnp.where(keep, value, 0.0)
                pieces.append(value)
            squares = pieces[0] * pieces[0]
            for piece in pieces[1:]:
                squares = squares + piece * piece
            square_ref[8 * first : 8 * first + 8, :] += squares
            highs[half] = jnp.concatenate(pieces, axis=1)
        value = jnp.concatenate(highs, axis=0)
        high = value.astype(BF16)
        low = (value - high.astype(F32)).astype(BF16)
        level_ref[8 * g : 8 * g + 16, :] = high
        level_ref[128 + 8 * g : 128 + 8 * g + 16, :] = low
    level = level_ref[...]
    total_ref[...] += lax.dot_general(dose_ref[...], level, NT, preferred_element_type=F32)
    stack = jnp.concatenate(design_parts(cov_ref[...], plate_ref[...]), axis=0)
    design_ref[...] += lax.dot_general(stack, level, NT, preferred_element_type=F32)

    @pl.when(step == pl.num_programs(0) - 1)
    def _():
        wide = design_ref[0:64, :] + design_ref[64:128, :] + design_ref[128:192, :]
        proj = wide[:, :LANES] + wide[:, LANES:]
        squares = lax.dot_general(
            jnp.ones((8, LANES), F32), square_ref[...], NT,
            precision=exact_mode, preferred_element_type=F32,
        )
        lane = lane_ids((256, LANES))
        for x in range(4):
            rows = slice(256 * x, 256 * x + 256)
            cross = total_ref[rows, :LANES] + total_ref[rows, LANES:]
            dose_sq = jnp.sum(dsq_ref[rows, :], axis=1, keepdims=True)
            out_ref[x, 0:256, :] = jnp.where(lane == 96, dose_sq, cross)
            out_ref[x, 256:384, :] = dproj_ref[128 * x : 128 * x + 128, :]
            out_ref[x, 384:448, :] = proj
            out_ref[x, 448:456, :] = squares


def cross_products(bin_ids, table, dosages, covariates, plates, dose_proj, dose_sq):
    count, width = dosages.shape
    tile = 512
    whole = pl.BlockSpec(memory_space=pltpu.VMEM)
    return pl.pallas_call(
        cross_kernel,
        grid=(width // tile,),
        in_specs=[
            pl.BlockSpec((96, tile), lambda s: (0, s)),
            whole,
            pl.BlockSpec((count, tile), lambda s: (0, s)),
            pl.BlockSpec((COVARS, tile), lambda s: (0, s)),
            pl.BlockSpec((1, tile), lambda s: (0, s)),
            whole,
            whole,
        ],
        out_specs=whole,
        out_shape=jax.ShapeDtypeStruct((4, 456, LANES), F32),
        scratch_shapes=[
            pltpu.VMEM((256, tile), BF16),
            pltpu.VMEM((count, 256), F32),
            pltpu.VMEM((192, 256), F32),
            pltpu.VMEM((LANES, LANES), F32),
        ],
        compiler_params=vmem_params(32),
        name="cross_products",
    )(bin_ids, table, dosages, covariates, plates, dose_proj, dose_sq)


def regroup_kernel(parts_ref, out_ref):
    total = parts_ref[0] + parts_ref[1] + parts_ref[2] + parts_ref[3]
    for z in range(8):
        out_ref[z, 0:32, :] = total[32 * z : 32 * z + 32]
        out_ref[z, 32:48, :] = total[256 + 16 * z : 256 + 16 * z + 16]
        out_ref[z, 48:120, :] = total[384:456]


def regroup(parts):
    whole = pl.BlockSpec(memory_space=pltpu.VMEM)
    return pl.pallas_call(
        regroup_kernel,
        in_specs=[whole],
        out_specs=whole,
        out_shape=jax.ShapeDtypeStruct((8, 120, LANES), F32),
        compiler_params=vmem_params(16),
        name="regroup",
    )(parts)


def finish_kernel(freedom, parts_ref, inverse_ref, out_ref):
    total = parts_ref[0]
    for z in range(1, 8):
        total = total + parts_ref[z]
    cross, dose, proj, squares = total[0:32], total[32:48], total[48:112], total[112:113]
    inverse = inverse_ref[...]
    dot = functools.partial(
        lax.dot_general, precision=exact_mode, preferred_element_type=F32
    )
    expr_white = dot(inverse, proj, NN)
    dose_both = jnp.concatenate([dose[:, :64], dose[:, 64:]], axis=0)
    dose_white = dot(dose_both, inverse, NT)
    expr_norm = squares - jnp.sum(expr_white * expr_white, axis=0, keepdims=True)
    dose_norm = cross[:, 96:97] - jnp.sum(dose_white * dose_white, axis=1, keepdims=True)
    cross = cross - dot(dose_white, expr_white, NN)
    corr = cross * lax.rsqrt(dose_norm * expr_norm + tiny_eps)
    stats = corr * jnp.sqrt(freedom / (1.0 - corr * corr))
    out_ref[...] = stats[:, : out_ref.shape[1]]


def finish(parts, inverse, freedom, proteins):
    whole = pl.BlockSpec(memory_space=pltpu.VMEM)
    return pl.pallas_call(
        functools.partial(finish_kernel, float(freedom)),
        in_specs=[whole, whole],
        out_specs=whole,
        out_shape=jax.ShapeDtypeStruct((32, proteins), F32),
        compiler_params=vmem_params(16),
        name="finish",
    )(parts, inverse)


def body(bin_ids, plate_ids, covariates, dosages):
    sample_total = bin_ids.shape[1] * lax.axis_size("samp")
    plates = plate_ids[None, :]
    x_groups = [[x * 8 + z for x in range(4)] for z in range(8)]
    z_groups = [[x * 8 + z for z in range(8)] for x in range(4)]
    base = (lax.axis_index("samp") * 24).astype(jnp.int32)[None]

    counts = histogram(bin_ids, covariates, plates).reshape(32, 24, LANES)
    counts = lax.all_to_all(counts, "samp", 0, 0, tiled=True)
    dose_proj, dose_sq = dose_products(dosages, covariates, plates)
    table = rank_table(counts, sample_total, base)
    table = lax.all_to_all(table, "samp", 0, 0, tiled=True).reshape(768, LANES)
    parts = cross_products(bin_ids, table, dosages, covariates, plates, dose_proj, dose_sq)
    gram = jnp.concatenate([table[736:, :64], table[736:, 64:]], axis=0)
    factor = lax.linalg.cholesky(gram, symmetrize_input=False)
    inverse = lax.linalg.triangular_solve(
        factor, jnp.eye(DESIGN, dtype=F32), left_side=True, lower=True
    )
    parts = lax.all_to_all(parts, "samp", 0, 0, axis_index_groups=x_groups, tiled=True)
    parts = regroup(parts)
    parts = lax.all_to_all(parts, "samp", 0, 0, axis_index_groups=z_groups, tiled=True)
    return finish(parts, inverse, sample_total - DESIGN - 1.0, bin_ids.shape[0])


def solution(mesh):
    placed = (P("prot", "samp"), P("samp"), P(None, "samp"), P(None, "samp"))
    return jax.shard_map(
        body, mesh=mesh, in_specs=placed, out_specs=P("samp", "prot"), check_vma=False
    )
```

time: 862 us -> 116 us (0.13)
  waiting for transfers between devices: 476 us -> 16.6 us
  blocking collectives: 208 us -> 14.4 us
  matrix products: 105 us -> 0.23 us
  Pallas kernels: 0 us -> 34 us
  starting transfers between devices: 0.08 us -> 24.6 us
  local copies, waits for them, and re-layouts: 25.8 us -> 11.9 us
  between operations: 13.3 us -> 0.09 us
  loops' own time: 11.2 us -> 0 us
  other arithmetic: 21.4 us -> 12.1 us
    psum x2 -> x0, waiting for transfers between devices: 258 us -> none  [the longest x1 130 us: body(): lax.psum((gram_part, dose_cross, dose_square), ('samp', 'prot'))]
    reduce_scatter x1 -> x0, waiting for transfers between devices: 218 us -> none  [body(): lax.psum_scatter(jnp.einsum('vs,ps->vp', dose_resid, expr_resid, precisio...]
    psum x2 -> x0, blocking collectives: 208 us -> none  [the longest x1 130 us: body(): expr_proj, expr_sq = lax.psum((expr_cross, expr_square), 'samp')]
    dot_general x23 -> x0, matrix products: 101 us -> none  [the longest x8 42.2 us: one_block(): jnp.einsum('pab,pbs->pas', table, lower_hot, precision=exact_mode, prefer...]
    pallas_call x0 -> x6, Pallas kernels: none -> 34 us  [the longest x1 12.9 us: cross_products(): pl.pallas_call(cross_kernel, grid=(width // tile,), in_specs=[pl.BlockSpe...]
    all_to_all x0 -> x3, starting transfers between devices: none -> 24.6 us  [the longest x1 11.6 us: body(): counts = lax.all_to_all(counts, 'samp', 0, 0, tiled=True)]
    all_to_all x0 -> x3, waiting for transfers between devices: none -> 16.6 us  [the longest x1 13.3 us: body(): counts = lax.all_to_all(counts, 'samp', 0, 0, tiled=True)]
    all_to_all x0 -> x1, blocking collectives: none -> 14.4 us  [body(): lax.all_to_all(parts, 'samp', 0, 0, axis_index_groups=x_groups, tiled=True)]
  transfers between devices with their start and end apart: 3 -> 3, of which waited for: 3 -> 3; matrix products, arithmetic and copies ran while one was open for 7% -> 11% of each run, Pallas kernels for 0% -> 5%
where the time goes in v1:
time: 116 us; the launch traced here: 114 us
  Pallas kernels  34 us (29%)
  starting transfers between devices  24.6 us (21%)
  waiting for transfers between devices  16.6 us (14%)
  blocking collectives  14.4 us (12%)
  other arithmetic  12.1 us (10%)
  local copies, waits for them, and re-layouts  11.9 us (10%)
    all_to_all x1, blocking collectives, body(): lax.all_to_all(parts, 'samp', 0, 0, axis_index_groups=x_groups, tiled=True)  14.4 us
    all_to_all x1, waiting for transfers between devices, body(): counts = lax.all_to_all(counts, 'samp', 0, 0, tiled=True)  13.3 us
    pallas_call x1, Pallas kernels, cross_products(): pl.pallas_call(cross_kernel, grid=(width // tile,), in_specs=[pl.BlockSpe...  12.9 us
    pallas_call x1, Pallas kernels, histogram(): pl.pallas_call(hist_kernel, grid=(12,), in_specs=[pl.BlockSpec((8, width)...  12.1 us
    unnamed x20, local copies, waits for them, and re-layouts  11.8 us
    all_to_all x1, starting transfers between devices, body(): counts = lax.all_to_all(counts, 'samp', 0, 0, tiled=True)  11.6 us
    all_to_all x1, starting transfers between devices, body(): lax.all_to_all(parts, 'samp', 0, 0, axis_index_groups=z_groups, tiled=True)  6.67 us
    another operation x3, other arithmetic, body(): factor = lax.linalg.cholesky(gram, symmetrize_input=False)  6.52 us
  transfers between devices with their start and end apart: 3, of which 3 were waited for; matrix products, arithmetic and copies ran while one was open for 11% of the time, Pallas kernels for 5%

profile of v1, /device:TPU:26, one launch (start us, length us, event | category | flops | bytes accessed | tf_op | source)
XLA Modules:
  0.0 113.9 jit_solution(7835227910354077610)
XLA Ops:
  0.0 0.0 copy-start.2
  0.0 1.4 %copy-done.2 = s32[92,4096]{1,0:T(8,128)S(1)} copy-done((s32[92,4096]{1,0:T(8,128)S(1)}, s32[92,4096]{1,0:T(8,128)}, u32[]{:S(2)}) %copy-start.2) | copy-done | bytes 1507352
  1.4 1.1 copy-done.4
  2.5 0.7 copy-done.7
  3.2 12.1 %histogram.1 = f32[768,128]{1,0:T(8,128)} custom-call(s32[92,4096]{1,0:T(8,128)S(1)} %copy-done.2, f32[40,4096]{1,0:T(8,128)S(1)} %copy-done.4, s32[1,4096]{1,0:T(1,128)S(1)} %bitcast.11), custom_call_target="tpu_custom_call" | custom-call | tf_op jit(solution)/shard_map/histogram/pallas_call | solution.py:96
  15.3 11.6 %all-to-all-start = ((f32[32,24,128]{2,1,0:T(8,128)}), f32[32,24,128]{2,1,0:T(8,128)S(1)}, u32[]{:S(2)}, u32[]{:S(2)}) async-start(f32[32,24,128]{2,1,0:T(8,128)} %bitcast.2), calls=%async_computation | async-start | bytes 786432 | tf_op jit(solution)/shard_map/all_to_all | solution.py:380
  26.9 13.3 %all-to-all-done.parts_ref = f32[32,24,128]{2,1,0:T(8,128)S(1)} async-done(((f32[32,24,128]{2,1,0:T(8,128)}), f32[32,24,128]{2,1,0:T(8,128)S(1)}, u32[]{:S(2)}, u32[]{:S(2)}) %all-to-all-start) | async-done | bytes 393248 | tf_op jit(solution)/shard_map/all_to_all | solution.py:380
  40.3 1.1 rank_table.1
  41.4 6.3 %all-to-all-start.1 = ((f32[32,24,128]{2,1,0:T(8,128)}), f32[32,24,128]{2,1,0:T(8,128)S(1)}, u32[]{:S(2)}, u32[]{:S(2)}) async-start(f32[32,24,128]{2,1,0:T(8,128)} %rank_table.1), calls=%async_computation.1 | async-start | bytes 786432 | tf_op jit(solution)/shard_map/all_to_all | solution.py:383
  47.7 0.0 copy-start
  47.7 3.4 %copy-done = bf16[1024,4096]{1,0:T(8,128)(2,1)S(1)} copy-done((bf16[1024,4096]{1,0:T(8,128)(2,1)S(1)}, bf16[1024,4096]{1,0:T(8,128)(2,1)}, u32[]{:S(2)}) %copy-start) | copy-done | bytes 8388632
  51.1 1.1 copy-done.5
  52.2 0.7 copy-done.8
  52.9 6.0 %dose_products.1 = (f32[512,128]{1,0:T(8,128)S(1)}, f32[1024,128]{1,0:T(8,128)S(1)}) custom-call(bf16[1024,4096]{1,0:T(8,128)(2,1)S(1)} %copy-done, f32[40,4096]{1,0:T(8,128)S(1)} %copy-done.5, s32[1,4096]{1,0:T(1,128)S(1)} %bitcast.12), custom_call_target="tpu_custom_call" | custom-call | flops 2147483648 | bytes 8388608 | tf_op jit(solution)/shard_map/dose_products/pallas_call | solution.py:145
  58.9 1.5 %all-to-all-done.1 = f32[32,24,128]{2,1,0:T(8,128)S(1)} async-done(((f32[32,24,128]{2,1,0:T(8,128)}), f32[32,24,128]{2,1,0:T(8,128)S(1)}, u32[]{:S(2)}, u32[]{:S(2)}) %all-to-all-start.1) | async-done | bytes 393248 | tf_op jit(solution)/shard_map/all_to_all | solution.py:383
  60.4 0.0 copy-done.3
  60.4 0.0 copy-done.6
  60.5 0.0 copy-done.9
  60.5 0.0 copy-start.1
  60.5 3.4 %copy-done.1 = bf16[1024,4096]{1,0:T(8,128)(2,1)S(1)} copy-done((bf16[1024,4096]{1,0:T(8,128)(2,1)S(1)}, bf16[1024,4096]{1,0:T(8,128)(2,1)}, u32[]{:S(2)}) %copy-start.1) | copy-done | bytes 8388632
  63.8 12.9 %cross_products.1 = f32[4,456,128]{2,1,0:T(8,128)S(1)} custom-call(s32[92,4096]{1,0:T(8,128)S(1)} %copy-done.3, f32[768,128]{1,0:T(8,128)S(1)} %bitcast.9, bf16[1024,4096]{1,0:T(8,128)(2,1)S(1)} %copy-done.1, f32[40,4096]{1,0:T(8,128)S(1)} %copy-done.6, s32[1,4096]{1,0:T(1,128)S(1)} %bitcast.13, f32[512,128]{1,0:T(8,128)S(1)} %get-tuple-element.7.dproj_ref, ...), custom_call_target="tpu_custom_call" | custom-call | tf_op jit(solution)/shard_map/cross_products/pallas_call | solution.py:295
  76.8 14.4 %all_to_all.20.parts_ref = f32[4,456,128]{2,1,0:T(8,128)S(1)} all-to-all(f32[4,456,128]{2,1,0:T(8,128)S(1)} %cross_products.1), channel_id=1, replica_groups={{0,64,128,192},{8,72,136,200},{16,80,144,208},{24,88,152,216},{32,96,16..., dimensions={0} | all-to-all | bytes 1867776 | tf_op jit(solution)/shard_map/all_to_all | solution.py:390
  91.1 0.8 regroup.1
  92.0 6.7 %all-to-all-start.3 = ((f32[8,120,128]{2,1,0:T(8,128)}), f32[8,120,128]{2,1,0:T(8,128)S(1)}, u32[]{:S(2)}, u32[]{:S(2)}) async-start(f32[8,120,128]{2,1,0:T(8,128)} %regroup.1), calls=%async_computation.3 | async-start | bytes 983040 | tf_op jit(solution)/shard_map/all_to_all | solution.py:392
  98.6 0.1 fusion.3
  98.7 5.8 %cholesky.17 = f32[64,64]{1,0:T(8,128)S(1)} custom-call(f32[64,64]{1,0:T(8,128)S(1)} %pad_maximum_fusion), custom_call_target="Cholesky" | custom-call | tf_op jit(solution)/shard_map/cholesky | solution.py:386
  104.6 0.6 compare_reduce_fusion
  105.2 0.7 fusion
  105.9 4.9 %custom-call.5 = f32[1,64,64]{1,2,0:T(8,128)S(1)} custom-call(f32[1,64,64]{2,1,0:T(8,128)S(1)} %fusion), custom_call_target="InvertDiagBlocksLowerTriangular" | custom-call | tf_op jit(solution)/shard_map/triangular_solve | solution.py:387
  110.8 0.2 fusion.1.inverse_ref
  111.0 1.8 %all-to-all-done.3.parts_ref = f32[8,120,128]{2,1,0:T(8,128)S(1)} async-done(((f32[8,120,128]{2,1,0:T(8,128)}), f32[8,120,128]{2,1,0:T(8,128)S(1)}, u32[]{:S(2)}, u32[]{:S(2)}) %all-to-all-start.3) | async-done | bytes 491552 | tf_op jit(solution)/shard_map/all_to_all | solution.py:392
  112.8 1.1 finish.1
  (9 shorter events, 0.0 us)
Async XLA Ops:
  0.0 1.4 %copy-start.2 = (s32[92,4096]{1,0:T(8,128)S(1)}, s32[92,4096]{1,0:T(8,128)}, u32[]{:S(2)}) copy-start(s32[92,4096]{1,0:T(8,128)} %bins_ref.3) | copy-start | bytes 4521988
  1.4 1.1 copy-start.4
  2.5 0.7 copy-start.7
  3.2 57.2 %copy-start.3 = (s32[92,4096]{1,0:T(8,128)S(1)}, s32[92,4096]{1,0:T(8,128)}, u32[]{:S(2)}) copy-start(s32[92,4096]{1,0:T(8,128)} %bins_ref.3) | copy-start | bytes 4521988
  3.2 57.2 %copy-start.6 = (f32[40,4096]{1,0:T(8,128)S(1)}, f32[40,4096]{1,0:T(8,128)}, u32[]{:S(2)}) copy-start(f32[40,4096]{1,0:T(8,128)} %cov_ref.5) | copy-start | bytes 1966084
  3.2 57.2 %copy-start.9 = (s32[4096]{0:T(1024)S(1)}, s32[4096]{0:T(1024)}, u32[]{:S(2)}) copy-start(s32[4096]{0:T(1024)} %param.5) | copy-start | bytes 49156
  15.3 25.0 %all-to-all-start = ((f32[32,24,128]{2,1,0:T(8,128)}), f32[32,24,128]{2,1,0:T(8,128)S(1)}, u32[]{:S(2)}, u32[]{:S(2)}) async-start(f32[32,24,128]{2,1,0:T(8,128)} %bitcast.2), calls=%async_computation | async-start | bytes 786432 | tf_op jit(solution)/shard_map/all_to_all | solution.py:380
  41.4 19.1 %all-to-all-start.1 = ((f32[32,24,128]{2,1,0:T(8,128)}), f32[32,24,128]{2,1,0:T(8,128)S(1)}, u32[]{:S(2)}, u32[]{:S(2)}) async-start(f32[32,24,128]{2,1,0:T(8,128)} %rank_table.1), calls=%async_computation.1 | async-start | bytes 786432 | tf_op jit(solution)/shard_map/all_to_all | solution.py:383
  47.7 3.4 %copy-start = (bf16[1024,4096]{1,0:T(8,128)(2,1)S(1)}, bf16[1024,4096]{1,0:T(8,128)(2,1)}, u32[]{:S(2)}) copy-start(bf16[1024,4096]{1,0:T(8,128)(2,1)} %dose_ref.3) | copy-start | bytes 25165828
  51.1 1.1 copy-start.5
  52.2 0.7 copy-start.8
  60.5 3.4 %copy-start.1 = (bf16[1024,4096]{1,0:T(8,128)(2,1)S(1)}, bf16[1024,4096]{1,0:T(8,128)(2,1)}, u32[]{:S(2)}) copy-start(bf16[1024,4096]{1,0:T(8,128)(2,1)} %dose_ref.3) | copy-start | bytes 25165828
  92.0 20.8 %all-to-all-start.3 = ((f32[8,120,128]{2,1,0:T(8,128)}), f32[8,120,128]{2,1,0:T(8,128)S(1)}, u32[]{:S(2)}, u32[]{:S(2)}) async-start(f32[8,120,128]{2,1,0:T(8,128)} %regroup.1), calls=%async_computation.3 | async-start | bytes 983040 | tf_op jit(solution)/shard_map/all_to_all | solution.py:392

commit v2 on v1

v2 whole, which is shorter than its diff:
```python
import functools
import math

import jax
import jax.numpy as jnp
from jax import lax
from jax.experimental import pallas as pl
from jax.experimental.pallas import tpu as pltpu
from jax.sharding import PartitionSpec as P

BINS = 1024
PLATES = 24
COVARS = 40
DESIGN = 64
DOSE_CHUNK = 1024
CROSS_CHUNK = 1024
LANES = 128
tiny_eps = 1e-06
F32 = jnp.float32
BF16 = jnp.bfloat16
FP8 = jnp.float8_e4m3fn
exact_mode = lax.Precision.HIGHEST
NT = (((1,), (1,)), ((), ()))
NN = (((1,), (0,)), ((), ()))


def vmem_params(mib):
    return pltpu.CompilerParams(vmem_limit_bytes=mib * 1024 * 1024)


def lane_ids(shape):
    return lax.broadcasted_iota(jnp.int32, shape, len(shape) - 1)


def design_parts(cov, plates):
    width = cov.shape[1]
    rows = lax.broadcasted_iota(jnp.int32, (PLATES, width), 0)
    plate_rows = jnp.where(plates == rows, 1.0, 0.0).astype(F32)
    design = jnp.concatenate([cov, plate_rows], axis=0)
    high = design.astype(BF16)
    rest = design - high.astype(F32)
    middle = rest.astype(BF16)
    low = (rest - middle.astype(F32)).astype(BF16)
    return high, middle, low


def fold_lanes(wide):
    first, second = wide[:, :LANES], wide[:, LANES:]
    pair = first + second
    return pair + pltpu.roll(pair, 64, 1)


WAITS = {0: (0, 1), 2: tuple(range(2, 14))}


def hist_kernel(bins_hbm, cov_hbm, plate_hbm, out_ref, bins_ref, cov_ref, plate_ref, table_ref, sems):
    proteins, width = bins_hbm.shape
    chunk = 1024
    groups = [(start, min(8, proteins - start)) for start in range(0, proteins, 8)]
    copies = [
        pltpu.make_async_copy(
            bins_hbm.at[pl.ds(start, size)], bins_ref.at[pl.ds(start, size)], sems.at[n]
        )
        for n, (start, size) in enumerate(groups)
    ]
    copies.append(pltpu.make_async_copy(cov_hbm, cov_ref, sems.at[len(groups)]))
    copies.append(pltpu.make_async_copy(plate_hbm, plate_ref, sems.at[len(groups) + 1]))
    for copy in copies:
        copy.start()
    ids = lax.broadcasted_iota(jnp.int32, (32, chunk), 0).astype(jnp.int8)
    one = jnp.ones((32, chunk), F32).astype(FP8)
    zero = jnp.zeros((32, chunk), F32).astype(FP8)
    block = lane_ids((8, LANES)) // 32
    for n, (first, size) in enumerate(groups):
        for k in WAITS.get(n, ()):
            copies[k].wait()
        side = 32 * size
        total = jnp.zeros((side, side), F32)
        for start in range(0, width, chunk):
            bins = bins_ref[first : first + size, start : start + chunk]
            left, right = [], []
            for p in range(size):
                row = jnp.broadcast_to(bins[p : p + 1], (32, chunk))
                left.append(jnp.where((row >> 5).astype(jnp.int8) == ids, one, zero))
                right.append(jnp.where((row & 31).astype(jnp.int8) == ids, one, zero))
            total = total + lax.dot_general(
                jnp.concatenate(left, axis=0),
                jnp.concatenate(right, axis=0),
                NT,
                preferred_element_type=F32,
            )
        lane = lane_ids((32, side)) // 32
        diag = total[:32]
        for p in range(1, size):
            diag = jnp.where(lane == p, total[32 * p : 32 * p + 32], diag)
        for half in range(side // LANES):
            table_ref[n % 2, half] = diag[:, half * LANES : (half + 1) * LANES]
            rows = [table_ref[n % 2, half, pl.ds(c, 8, stride=4), :] for c in range(4)]
            for q in range(4):
                out = rows[q]
                for c in range(4):
                    shift = ((c - q) % 4) * 32
                    moved = pltpu.roll(rows[c], shift, 1) if shift else rows[c]
                    out = jnp.where(block == c, moved, out)
                p = first + half * 4 + q
                out_ref[8 * p : 8 * p + 8, :] = out
    high, middle, low = design_parts(cov_ref[...], plate_ref[...])
    stack = jnp.concatenate([high, middle, low, jnp.zeros_like(high)], axis=0)
    wide = lax.dot_general(stack[:192], stack, NT, preferred_element_type=F32)
    gram = fold_lanes(wide[:64] + wide[64:128] + wide[128:192])
    out_ref[8 * proteins :, :] = jnp.where(lane_ids((32, LANES)) < 64, gram[:32], gram[32:])


def histogram(bin_ids, covariates, plates):
    proteins, width = bin_ids.shape
    hbm = pl.BlockSpec(memory_space=pl.ANY)
    return pl.pallas_call(
        hist_kernel,
        in_specs=[hbm, hbm, hbm],
        out_specs=pl.BlockSpec(memory_space=pltpu.VMEM),
        out_shape=jax.ShapeDtypeStruct((768, LANES), F32),
        scratch_shapes=[
            pltpu.VMEM((96, width), jnp.int32),
            pltpu.VMEM((COVARS, width), F32),
            pltpu.VMEM((1, width), jnp.int32),
            pltpu.VMEM((2, 2, 32, LANES), F32),
            pltpu.SemaphoreType.DMA((14,)),
        ],
        compiler_params=vmem_params(60),
        name="histogram",
    )(bin_ids, covariates, plates)


def dose_kernel(dose_hbm, cov_ref, plate_ref, proj_ref, square_ref, dose_ref, total_ref, part_ref, sems):
    chunk = dose_ref.shape[2]
    copies = [
        pltpu.make_async_copy(
            dose_hbm.at[:, pl.ds(c * chunk, chunk)], dose_ref.at[c], sems.at[c]
        )
        for c in range(dose_ref.shape[0])
    ]
    for copy in copies:
        copy.start()
    high, middle, low = design_parts(cov_ref[...], plate_ref[...])
    stack = jnp.concatenate([high, middle, low, jnp.zeros_like(high)], axis=0)
    for c in range(len(copies)):
        copies[c].wait()
        for r in range(0, dose_ref.shape[1], 256):
            dose = dose_ref[c, r : r + 256, :]
            term = lax.dot_general(
                dose, stack[:, c * chunk : (c + 1) * chunk], NT, preferred_element_type=F32
            )
            wide = dose.astype(F32)
            wide = wide * wide
            part = wide[:, :LANES]
            for start in range(LANES, chunk, LANES):
                part = part + wide[:, start : start + LANES]
            if c == 0:
                total_ref[r : r + 256, :] = term
                part_ref[r : r + 256, :] = part
            else:
                total_ref[r : r + 256, :] += term
                part_ref[r : r + 256, :] += part
    half = lane_ids((16, LANES)) < 64
    for c in range(32):
        both = fold_lanes(total_ref[32 * c : 32 * c + 32, :])
        proj_ref[16 * c : 16 * c + 16, :] = jnp.where(half, both[:16], both[16:])
    squares = lax.dot_general(
        jnp.ones((8, LANES), F32), part_ref[...], NT,
        precision=exact_mode, preferred_element_type=F32,
    )
    for c in range(8):
        square_ref[c : c + 1, :] = squares[0:1, LANES * c : LANES * (c + 1)]


def dose_products(dosages, covariates, plates):
    count, width = dosages.shape
    chunk = DOSE_CHUNK
    whole = pl.BlockSpec(memory_space=pltpu.VMEM)
    return pl.pallas_call(
        dose_kernel,
        in_specs=[pl.BlockSpec(memory_space=pl.ANY), whole, whole],
        out_specs=[whole, whole],
        out_shape=[
            jax.ShapeDtypeStruct((count // 2, LANES), F32),
            jax.ShapeDtypeStruct((8, LANES), F32),
        ],
        scratch_shapes=[
            pltpu.VMEM((width // chunk, count, chunk), BF16),
            pltpu.VMEM((count, 256), F32),
            pltpu.VMEM((count, LANES), F32),
            pltpu.SemaphoreType.DMA((width // chunk,)),
        ],
        compiler_params=vmem_params(60),
        cost_estimate=pl.CostEstimate(
            flops=2 * count * width * 256, bytes_accessed=count * width * 2, transcendentals=0
        ),
        name="dose_products",
    )(dosages, covariates, plates)


def erf_inverse(x):
    w = -jnp.log1p(-x * x)
    small = w < 5.0
    shifted = jnp.where(small, w - 2.5, jnp.sqrt(w) - 3.0)
    near = (
        2.81022636e-08, 3.43273939e-07, -3.5233877e-06, -4.39150654e-06, 0.00021858087,
        -0.00125372503, -0.00417768164, 0.246640727, 1.50140941,
    )
    far = (
        -0.000200214257, 0.000100950558, 0.00134934322, -0.00367342844, 0.00573950773,
        -0.0076224613, 0.00943887047, 1.00167406, 2.83297682,
    )
    value = jnp.where(small, near[0], far[0])
    for a, b in zip(near[1:], far[1:]):
        value = value * shifted + jnp.where(small, a, b)
    return value * x


def table_kernel(sample_total, base_ref, parts_ref, out_ref):
    counts = jnp.sum(parts_ref[...], axis=0)
    rows = counts.shape[0]
    row = lax.broadcasted_iota(jnp.int32, (LANES, LANES), 0)
    before = (row < lane_ids((LANES, LANES))).astype(F32)
    inside = lax.dot_general(
        counts, before, NN, precision=exact_mode, preferred_element_type=F32
    )
    totals = jnp.broadcast_to(jnp.sum(counts, axis=1, keepdims=True), counts.shape)
    row = lax.broadcasted_iota(jnp.int32, (rows, rows), 0)
    col = lane_ids((rows, rows))
    earlier = ((col < row) & (col // 8 == row // 8)).astype(F32)
    outside = lax.dot_general(
        earlier, totals, NN, precision=exact_mode, preferred_element_type=F32
    )
    middle = inside + outside + 0.5 * (counts + 1.0)
    level = (middle - 0.375) / (sample_total + 0.25)
    values = math.sqrt(2.0) * erf_inverse(2.0 * level - 1.0)
    place = base_ref[0] + lax.broadcasted_iota(jnp.int32, counts.shape, 0)
    values = jnp.where(place < 736, values, counts)
    for n in range(out_ref.shape[0]):
        out_ref[n] = values


def rank_table(parts, sample_total, base):
    return pl.pallas_call(
        functools.partial(table_kernel, float(sample_total)),
        in_specs=[
            pl.BlockSpec(memory_space=pltpu.SMEM),
            pl.BlockSpec(memory_space=pltpu.VMEM),
        ],
        out_specs=pl.BlockSpec(memory_space=pltpu.VMEM),
        out_shape=jax.ShapeDtypeStruct(parts.shape, F32),
        compiler_params=vmem_params(16),
        name="rank_table",
    )(base, parts)


def lookup(bins, tables):
    lower = bins & 127
    values = [
        jnp.take_along_axis(table, lower, axis=1, mode="promise_in_bounds") for table in tables
    ]
    for bit in (128, 256, 512):
        odd = (bins & bit) != 0
        values = [jnp.where(odd, values[i + 1], values[i]) for i in range(0, len(values), 2)]
    return values[0]


def cross_kernel(
    bins_hbm, table_ref, dose_hbm, cov_hbm, plate_hbm, dproj_ref, dsq_ref,
    out_ref, bins_ref, cov_ref, plate_ref, dose_ref, level_ref, total_ref, design_ref, square_ref, sems,
):
    proteins, width = bins_hbm.shape
    chunk = dose_ref.shape[2]
    steps = width // chunk
    spans = [pl.ds(c * chunk, chunk) for c in range(steps)]
    bins_in = [
        pltpu.make_async_copy(
            bins_hbm.at[:, spans[c]], bins_ref.at[c], sems.at[c]
        )
        for c in range(steps)
    ]
    dose_in = [
        pltpu.make_async_copy(dose_hbm.at[:, spans[c]], dose_ref.at[c], sems.at[steps + c])
        for c in range(steps)
    ]
    rest_in = [
        pltpu.make_async_copy(cov_hbm, cov_ref, sems.at[2 * steps]),
        pltpu.make_async_copy(plate_hbm, plate_ref, sems.at[2 * steps + 1]),
    ]
    for copy in [bins_in[0], bins_in[1]] + rest_in + [dose_in[0]] + bins_in[2:] + dose_in[1:]:
        copy.start()
    square_ref[...] = jnp.zeros_like(square_ref)
    for c in range(steps):
        level_ref[c, 96:128, :] = jnp.zeros((32, chunk), BF16)
        level_ref[c, 224:256, :] = jnp.zeros((32, chunk), BF16)

    def levels(c):
        for g in range(0, 12, 2):
            pair = []
            for first in (g, g + 1):
                size = min(8, proteins - 8 * first)
                tables = [table_ref[pl.ds(64 * first + k, size, stride=8), :] for k in range(8)]
                pieces, squares = [], None
                for start in range(0, chunk, LANES):
                    bins = bins_ref[c, 8 * first : 8 * first + size, start : start + LANES]
                    value = lookup(bins, tables)
                    pieces.append(value)
                    squares = value * value if squares is None else squares + value * value
                square_ref[8 * first : 8 * first + size, :] += squares
                pieces = jnp.concatenate(pieces, axis=1)
                if size < 8:
                    pieces = jnp.concatenate([pieces, jnp.zeros((8 - size, chunk), F32)], axis=0)
                pair.append(pieces)
            value = jnp.concatenate(pair, axis=0)
            high = value.astype(BF16)
            low = (value - high.astype(F32)).astype(BF16)
            level_ref[c, 8 * g : 8 * g + 16, :] = high
            level_ref[c, 128 + 8 * g : 128 + 8 * g + 16, :] = low

    bins_in[0].wait()
    levels(0)
    for c in range(steps):
        dose_in[c].wait()
        if c == 0:
            for copy in rest_in:
                copy.wait()
        if c + 1 < steps:
            bins_in[c + 1].wait()
            levels(c + 1)
        level = level_ref[c]
        span = slice(c * chunk, (c + 1) * chunk)
        stack = jnp.concatenate(design_parts(cov_ref[:, span], plate_ref[:, span]), axis=0)
        design = lax.dot_general(stack, level, NT, preferred_element_type=F32)
        total = lax.dot_general(dose_ref[c], level, NT, preferred_element_type=F32)
        if c == 0:
            design_ref[...] = design
            total_ref[...] = total
        else:
            design_ref[...] += design
            total_ref[...] += total
    wide = design_ref[0:64, :] + design_ref[64:128, :] + design_ref[128:192, :]
    proj = wide[:, :LANES] + wide[:, LANES:]
    squares = lax.dot_general(
        jnp.ones((8, LANES), F32), square_ref[...], NT,
        precision=exact_mode, preferred_element_type=F32,
    )
    for x in range(4):
        rows = slice(256 * x, 256 * x + 256)
        out_ref[x, 0:256, :] = total_ref[rows, :LANES] + total_ref[rows, LANES:]
        out_ref[x, 256:384, :] = dproj_ref[128 * x : 128 * x + 128, :]
        out_ref[x, 384:448, :] = proj
        out_ref[x, 448:456, :] = squares
        out_ref[x, 450:452, :] = dsq_ref[2 * x : 2 * x + 2, :]


def cross_products(bin_ids, table, dosages, covariates, plates, dose_proj, dose_sq):
    count, width = dosages.shape
    chunk = CROSS_CHUNK
    steps = width // chunk
    whole = pl.BlockSpec(memory_space=pltpu.VMEM)
    hbm = pl.BlockSpec(memory_space=pl.ANY)
    return pl.pallas_call(
        cross_kernel,
        in_specs=[hbm, whole, hbm, hbm, hbm, whole, whole],
        out_specs=whole,
        out_shape=jax.ShapeDtypeStruct((4, 456, LANES), F32),
        scratch_shapes=[
            pltpu.VMEM((steps, bin_ids.shape[0], chunk), jnp.int32),
            pltpu.VMEM((COVARS, width), F32),
            pltpu.VMEM((1, width), jnp.int32),
            pltpu.VMEM((steps, count, chunk), BF16),
            pltpu.VMEM((steps, 256, chunk), BF16),
            pltpu.VMEM((count, 256), F32),
            pltpu.VMEM((192, 256), F32),
            pltpu.VMEM((LANES, LANES), F32),
            pltpu.SemaphoreType.DMA((2 * steps + 2,)),
        ],
        compiler_params=vmem_params(60),
        name="cross_products",
    )(bin_ids, table, dosages, covariates, plates, dose_proj, dose_sq)


def regroup_kernel(parts_ref, out_ref):
    total = parts_ref[0] + parts_ref[1] + parts_ref[2] + parts_ref[3]
    row = lax.broadcasted_iota(jnp.int32, (8, LANES), 0)
    for z in range(8):
        out_ref[z, 0:32, :] = total[32 * z : 32 * z + 32]
        out_ref[z, 32:48, :] = total[256 + 16 * z : 256 + 16 * z + 16]
        out_ref[z, 48:112, :] = total[384:448]
        squares = total[448:456]
        own = squares[2 + z // 4 : 3 + z // 4]
        own = pltpu.roll(own, (4 - z % 4) % 4 * 32, 1) if z % 4 else own
        out_ref[z, 112:120, :] = jnp.where(row == 1, own, squares)


def regroup(parts):
    whole = pl.BlockSpec(memory_space=pltpu.VMEM)
    return pl.pallas_call(
        regroup_kernel,
        in_specs=[whole],
        out_specs=whole,
        out_shape=jax.ShapeDtypeStruct((8, 120, LANES), F32),
        compiler_params=vmem_params(16),
        name="regroup",
    )(parts)


def finish_kernel(freedom, parts_ref, inverse_ref, out_ref):
    total = parts_ref[0]
    for z in range(1, 8):
        total = total + parts_ref[z]
    cross, dose, proj, squares = total[0:32], total[32:48], total[48:112], total[112:113]
    shape = (32, LANES)
    diagonal = lax.broadcasted_iota(jnp.int32, shape, 0) == lane_ids(shape)
    dose_squares = jnp.sum(
        jnp.where(diagonal, jnp.broadcast_to(total[113:114], shape), 0.0), axis=1, keepdims=True
    )
    inverse = inverse_ref[...]
    dot = functools.partial(
        lax.dot_general, precision=exact_mode, preferred_element_type=F32
    )
    expr_white = dot(inverse, proj, NN)
    dose_both = jnp.concatenate([dose[:, :64], dose[:, 64:]], axis=0)
    dose_white = dot(dose_both, inverse, NT)
    expr_norm = squares - jnp.sum(expr_white * expr_white, axis=0, keepdims=True)
    dose_norm = dose_squares - jnp.sum(dose_white * dose_white, axis=1, keepdims=True)
    cross = cross - dot(dose_white, expr_white, NN)
    corr = cross * lax.rsqrt(dose_norm * expr_norm + tiny_eps)
    stats = corr * jnp.sqrt(freedom / (1.0 - corr * corr))
    out_ref[...] = stats[:, : out_ref.shape[1]]


def finish(parts, inverse, freedom, proteins):
    whole = pl.BlockSpec(memory_space=pltpu.VMEM)
    return pl.pallas_call(
        functools.partial(finish_kernel, float(freedom)),
        in_specs=[whole, whole],
        out_specs=whole,
        out_shape=jax.ShapeDtypeStruct((32, proteins), F32),
        compiler_params=vmem_params(16),
        name="finish",
    )(parts, inverse)


def body(bin_ids, plate_ids, covariates, dosages):
    sample_total = bin_ids.shape[1] * lax.axis_size("samp")
    plates = plate_ids[None, :]
    x_groups = [[x * 8 + z for x in range(4)] for z in range(8)]
    z_groups = [[x * 8 + z for z in range(8)] for x in range(4)]
    base = (lax.axis_index("samp") * 24).astype(jnp.int32)[None]

    counts = histogram(bin_ids, covariates, plates).reshape(32, 24, LANES)
    counts = lax.all_to_all(counts, "samp", 0, 0, tiled=True)
    dose_proj, dose_sq = dose_products(dosages, covariates, plates)
    counts, dose_proj, dose_sq = lax.optimization_barrier((counts, dose_proj, dose_sq))
    table = rank_table(counts, sample_total, base)
    table = lax.all_to_all(table, "samp", 0, 0, tiled=True).reshape(768, LANES)
    parts = cross_products(bin_ids, table, dosages, covariates, plates, dose_proj, dose_sq)
    packed, parts = lax.optimization_barrier((table[736:], parts))
    gram = jnp.concatenate([packed[:, :64], packed[:, 64:]], axis=0)
    factor = lax.linalg.cholesky(gram, symmetrize_input=False)
    parts = lax.all_to_all(parts, "samp", 0, 0, axis_index_groups=x_groups, tiled=True)
    parts, factor = lax.optimization_barrier((parts, factor))
    inverse = lax.linalg.triangular_solve(
        factor, jnp.eye(DESIGN, dtype=F32), left_side=True, lower=True
    )
    parts = regroup(parts)
    parts = lax.all_to_all(parts, "samp", 0, 0, axis_index_groups=z_groups, tiled=True)
    return finish(parts, inverse, sample_total - DESIGN - 1.0, bin_ids.shape[0])


def solution(mesh):
    placed = (P("prot", "samp"), P("samp"), P(None, "samp"), P(None, "samp"))
    return jax.shard_map(
        body, mesh=mesh, in_specs=placed, out_specs=P("samp", "prot"), check_vma=False
    )
```

time: 116 us -> 97.7 us (0.84)
  local copies, waits for them, and re-layouts: 11.9 us -> 0.82 us
  Pallas kernels: 34 us -> 24.9 us
  blocking collectives: 14.4 us -> 18.9 us
  starting transfers between devices: 24.6 us -> 22.3 us
    unnamed x20 -> x2, local copies, waits for them, and re-layouts: 11.8 us -> 0.75 us
    pallas_call x3, Pallas kernels: 31 us -> 22.6 us  [the longest x1 9.43 us: cross_products(): pl.pallas_call(cross_kernel, in_specs=[hbm, whole, hbm, hbm, hbm, whole,...]
    all_to_all x1, waiting for transfers between devices: 1.77 us -> 8.53 us  [body(): lax.all_to_all(parts, 'samp', 0, 0, axis_index_groups=z_groups, tiled=True)]
    all_to_all x1, waiting for transfers between devices: 13.3 us -> 6.92 us  [body(): counts = lax.all_to_all(counts, 'samp', 0, 0, tiled=True)]
    all_to_all x1, blocking collectives: 14.4 us -> 18.9 us  [body(): table = lax.all_to_all(table, 'samp', 0, 0, tiled=True).reshape(768, LANES)]
    all_to_all x1, starting transfers between devices: 6.32 us -> 4.88 us  [body(): lax.all_to_all(parts, 'samp', 0, 0, axis_index_groups=x_groups, tiled=True)]
  transfers between devices with their start and end apart: 3 -> 3, of which waited for: 3 -> 3; matrix products, arithmetic and copies ran while one was open for 11% -> 13% of each run, Pallas kernels for 5% -> 7%
where the time goes in v2:
time: 97.7 us; the launch traced here: 96.3 us
  Pallas kernels  24.9 us (25%)
  starting transfers between devices  22.3 us (23%)
  blocking collectives  18.9 us (19%)
  waiting for transfers between devices  17 us (17%)
  other arithmetic  12.1 us (12%)
    all_to_all x1, blocking collectives, body(): table = lax.all_to_all(table, 'samp', 0, 0, tiled=True).reshape(768, LANES)  18.9 us
    all_to_all x1, starting transfers between devices, body(): counts = lax.all_to_all(counts, 'samp', 0, 0, tiled=True)  11.6 us
    pallas_call x1, Pallas kernels, cross_products(): pl.pallas_call(cross_kernel, in_specs=[hbm, whole, hbm, hbm, hbm, whole,...  9.43 us
    all_to_all x1, waiting for transfers between devices, body(): lax.all_to_all(parts, 'samp', 0, 0, axis_index_groups=z_groups, tiled=True)  8.53 us
    all_to_all x1, waiting for transfers between devices, body(): counts = lax.all_to_all(counts, 'samp', 0, 0, tiled=True)  6.92 us
    pallas_call x1, Pallas kernels, histogram(): pl.pallas_call(hist_kernel, in_specs=[hbm, hbm, hbm], out_specs=pl.BlockS...  6.77 us
    another operation x3, other arithmetic, body(): factor = lax.linalg.cholesky(gram, symmetrize_input=False)  6.52 us
    pallas_call x1, Pallas kernels, dose_products(): pl.pallas_call(dose_kernel, in_specs=[pl.BlockSpec(memory_space=pl.ANY),...  6.41 us
  transfers between devices with their start and end apart: 3, of which 3 were waited for; matrix products, arithmetic and copies ran while one was open for 13% of the time, Pallas kernels for 7%

profile of v2, /device:TPU:26, one launch (start us, length us, event | category | flops | bytes accessed | tf_op | source)
XLA Modules:
  0.0 96.3 jit_solution(15766471483579661134)
XLA Ops:
  0.0 6.8 %histogram.1 = f32[768,128]{1,0:T(8,128)} custom-call(s32[92,4096]{1,0:T(8,128)} %bins_hbm.3, f32[40,4096]{1,0:T(8,128)} %cov_hbm.3, s32[1,4096]{1,0:T(1,128)} %bitcast.12), custom_call_target="tpu_custom_call" | custom-call | tf_op jit(solution)/shard_map/histogram/pallas_call | solution.py:117
  6.8 11.6 %all-to-all-start = ((f32[32,24,128]{2,1,0:T(8,128)}), f32[32,24,128]{2,1,0:T(8,128)S(1)}, u32[]{:S(2)}, u32[]{:S(2)}) async-start(f32[32,24,128]{2,1,0:T(8,128)} %bitcast.11), calls=%async_computation | async-start | bytes 786432 | tf_op jit(solution)/shard_map/all_to_all | solution.py:454
  18.4 6.4 %dose_products.1 = (f32[512,128]{1,0:T(8,128)}, f32[8,128]{1,0:T(8,128)}) custom-call(bf16[1024,4096]{1,0:T(8,128)(2,1)} %dose_hbm.3, f32[40,4096]{1,0:T(8,128)} %cov_hbm.3, s32[1,4096]{1,0:T(1,128)} %bitcast.13), custom_call_target="tpu_custom_call" | custom-call | flops 2147483648 | bytes 8388608 | tf_op jit(solution)/shard_map/dose_products/pallas_call | solution.py:180
  24.8 6.9 %all-to-all-done.parts_ref = f32[32,24,128]{2,1,0:T(8,128)S(1)} async-done(((f32[32,24,128]{2,1,0:T(8,128)}), f32[32,24,128]{2,1,0:T(8,128)S(1)}, u32[]{:S(2)}, u32[]{:S(2)}) %all-to-all-start) | async-done | bytes 393248 | tf_op jit(solution)/shard_map/all_to_all | solution.py:454
  31.8 0.4 rank_table.1
  32.1 18.9 %all_to_all.20 = f32[32,24,128]{2,1,0:T(8,128)S(1)} all-to-all(f32[32,24,128]{2,1,0:T(8,128)S(1)} %rank_table.1), channel_id=1, replica_groups=mesh['samp'=32,'prot'=8] {'samp'}, dimensions={0} | all-to-all | bytes 786432 | tf_op jit(solution)/shard_map/all_to_all | solution.py:458
  51.0 0.0 copy-start
  51.0 0.7 copy-done
  51.8 9.4 %cross_products.1 = f32[4,456,128]{2,1,0:T(8,128)} custom-call(s32[92,4096]{1,0:T(8,128)} %bins_hbm.3, f32[768,128]{1,0:T(8,128)} %bitcast.10, bf16[1024,4096]{1,0:T(8,128)(2,1)} %dose_hbm.3, f32[40,4096]{1,0:T(8,128)} %cov_hbm.3, s32[1,4096]{1,0:T(1,128)} %bitcast.14, f32[512,128]{1,0:T(8,128)} %get-tuple-element.17.dproj_ref, ...), custom_call_target="tpu_custom_call" | custom-call | tf_op jit(solution)/shard_map/cross_products/pallas_call | solution.py:363
  61.2 4.9 %all-to-all-start.2 = ((f32[4,456,128]{2,1,0:T(8,128)}), f32[4,456,128]{2,1,0:T(8,128)S(1)}, u32[]{:S(2)}, u32[]{:S(2)}) async-start(f32[4,456,128]{2,1,0:T(8,128)} %cross_products.1), calls=%async_computation.2 | async-start | bytes 1867776 | tf_op jit(solution)/shard_map/all_to_all | solution.py:463
  66.1 0.1 fusion.2
  66.2 5.8 %cholesky.20 = f32[64,64]{1,0:T(8,128)S(1)} custom-call(f32[64,64]{1,0:T(8,128)S(1)} %pad_maximum_fusion), custom_call_target="Cholesky" | custom-call | tf_op jit(solution)/shard_map/cholesky | solution.py:462
  72.0 0.6 compare_reduce_fusion
  72.7 0.7 select_select_fusion
  73.3 1.6 %all-to-all-done.2.parts_ref = f32[4,456,128]{2,1,0:T(8,128)S(1)} async-done(((f32[4,456,128]{2,1,0:T(8,128)}), f32[4,456,128]{2,1,0:T(8,128)S(1)}, u32[]{:S(2)}, u32[]{:S(2)}) %all-to-all-start.2) | async-done | bytes 933920 | tf_op jit(solution)/shard_map/all_to_all | solution.py:463
  74.9 0.8 regroup.1
  75.7 5.8 %all-to-all-start.3 = ((f32[8,120,128]{2,1,0:T(8,128)}), f32[8,120,128]{2,1,0:T(8,128)S(1)}, u32[]{:S(2)}, u32[]{:S(2)}) async-start(f32[8,120,128]{2,1,0:T(8,128)} %regroup.1), calls=%async_computation.3 | async-start | bytes 983040 | tf_op jit(solution)/shard_map/all_to_all | solution.py:469
  81.6 4.9 %custom-call.5 = f32[1,64,64]{1,2,0:T(8,128)S(1)} custom-call(f32[1,64,64]{2,1,0:T(8,128)S(1)} %select_bitcast_fusion), custom_call_target="InvertDiagBlocksLowerTriangular" | custom-call | tf_op jit(solution)/shard_map/triangular_solve | solution.py:465
  86.5 0.2 fusion.inverse_ref
  86.7 8.5 %all-to-all-done.3.parts_ref = f32[8,120,128]{2,1,0:T(8,128)S(1)} async-done(((f32[8,120,128]{2,1,0:T(8,128)}), f32[8,120,128]{2,1,0:T(8,128)S(1)}, u32[]{:S(2)}, u32[]{:S(2)}) %all-to-all-start.3) | async-done | bytes 491552 | tf_op jit(solution)/shard_map/all_to_all | solution.py:469
  95.3 1.1 %finish.1 = f32[32,92]{1,0:T(8,128)} custom-call(f32[8,120,128]{2,1,0:T(8,128)S(1)} %all-to-all-done.3.parts_ref, f32[64,64]{1,0:T(8,128)S(1)} %fusion.inverse_ref), custom_call_target="tpu_custom_call" | custom-call | tf_op jit(solution)/shard_map/finish/pallas_call | solution.py:436
  (4 shorter events, 0.0 us)
Async XLA Ops:
  6.8 25.0 %all-to-all-start = ((f32[32,24,128]{2,1,0:T(8,128)}), f32[32,24,128]{2,1,0:T(8,128)S(1)}, u32[]{:S(2)}, u32[]{:S(2)}) async-start(f32[32,24,128]{2,1,0:T(8,128)} %bitcast.11), calls=%async_computation | async-start | bytes 786432 | tf_op jit(solution)/shard_map/all_to_all | solution.py:454
  51.0 0.8 copy-start
  61.2 13.7 %all-to-all-start.2 = ((f32[4,456,128]{2,1,0:T(8,128)}), f32[4,456,128]{2,1,0:T(8,128)S(1)}, u32[]{:S(2)}, u32[]{:S(2)}) async-start(f32[4,456,128]{2,1,0:T(8,128)} %cross_products.1), calls=%async_computation.2 | async-start | bytes 1867776 | tf_op jit(solution)/shard_map/all_to_all | solution.py:463
  75.7 19.5 %all-to-all-start.3 = ((f32[8,120,128]{2,1,0:T(8,128)}), f32[8,120,128]{2,1,0:T(8,128)S(1)}, u32[]{:S(2)}, u32[]{:S(2)}) async-start(f32[8,120,128]{2,1,0:T(8,128)} %regroup.1), calls=%async_computation.3 | async-start | bytes 983040 | tf_op jit(solution)/shard_map/all_to_all | solution.py:469

commit v3 on v2

--- a/solution.py
+++ b/solution.py
@@ -131,7 +131,7 @@
     )(bin_ids, covariates, plates)
 
 
-def dose_kernel(dose_hbm, cov_ref, plate_ref, proj_ref, square_ref, dose_ref, total_ref, part_ref, sems):
+def dose_kernel(dose_hbm, cov_ref, plate_ref, proj_ref, dose_ref, total_ref, part_ref, sems):
     chunk = dose_ref.shape[2]
     copies = [
         pltpu.make_async_copy(
@@ -161,16 +161,14 @@
             else:
                 total_ref[r : r + 256, :] += term
                 part_ref[r : r + 256, :] += part
-    half = lane_ids((16, LANES)) < 64
-    for c in range(32):
-        both = fold_lanes(total_ref[32 * c : 32 * c + 32, :])
-        proj_ref[16 * c : 16 * c + 16, :] = jnp.where(half, both[:16], both[16:])
+    for c in range(proj_ref.shape[1] // LANES):
+        span = slice(LANES * c, LANES * (c + 1))
+        proj_ref[0:64, span] = fold_lanes(total_ref[span, :]).T[:64]
     squares = lax.dot_general(
         jnp.ones((8, LANES), F32), part_ref[...], NT,
         precision=exact_mode, preferred_element_type=F32,
     )
-    for c in range(8):
-        square_ref[c : c + 1, :] = squares[0:1, LANES * c : LANES * (c + 1)]
+    proj_ref[64:72, :] = squares
 
 
 def dose_products(dosages, covariates, plates):
@@ -180,18 +178,15 @@
     return pl.pallas_call(
         dose_kernel,
         in_specs=[pl.BlockSpec(memory_space=pl.ANY), whole, whole],
-        out_specs=[whole, whole],
-        out_shape=[
-            jax.ShapeDtypeStruct((count // 2, LANES), F32),
-            jax.ShapeDtypeStruct((8, LANES), F32),
-        ],
+        out_specs=whole,
+        out_shape=jax.ShapeDtypeStruct((DESIGN + 8, count), F32),
         scratch_shapes=[
             pltpu.VMEM((width // chunk, count, chunk), BF16),
             pltpu.VMEM((count, 256), F32),
             pltpu.VMEM((count, LANES), F32),
             pltpu.SemaphoreType.DMA((width // chunk,)),
         ],
-        compiler_params=vmem_params(60),
+        compiler_params=vmem_params(50),
         cost_estimate=pl.CostEstimate(
             flops=2 * count * width * 256, bytes_accessed=count * width * 2, transcendentals=0
         ),
@@ -250,7 +245,7 @@
         ],
         out_specs=pl.BlockSpec(memory_space=pltpu.VMEM),
         out_shape=jax.ShapeDtypeStruct(parts.shape, F32),
-        compiler_params=vmem_params(16),
+        compiler_params=vmem_params(8),
         name="rank_table",
     )(base, parts)
 
@@ -267,7 +262,7 @@
 
 
 def cross_kernel(
-    bins_hbm, table_ref, dose_hbm, cov_hbm, plate_hbm, dproj_ref, dsq_ref,
+    bins_hbm, table_ref, dose_hbm, cov_hbm, plate_hbm, dproj_ref,
     out_ref, bins_ref, cov_ref, plate_ref, dose_ref, level_ref, total_ref, design_ref, square_ref, sems,
 ):
     proteins, width = bins_hbm.shape
@@ -345,16 +340,23 @@
         jnp.ones((8, LANES), F32), square_ref[...], NT,
         precision=exact_mode, preferred_element_type=F32,
     )
+    spare = lane_ids((64, LANES)) >= 96
+    own = [pltpu.roll(squares[0:1], shift, 1) for shift in (96, 64, 32)]
     for x in range(4):
         rows = slice(256 * x, 256 * x + 256)
         out_ref[x, 0:256, :] = total_ref[rows, :LANES] + total_ref[rows, LANES:]
-        out_ref[x, 256:384, :] = dproj_ref[128 * x : 128 * x + 128, :]
-        out_ref[x, 384:448, :] = proj
-        out_ref[x, 448:456, :] = squares
-        out_ref[x, 450:452, :] = dsq_ref[2 * x : 2 * x + 2, :]
-
-
-def cross_products(bin_ids, table, dosages, covariates, plates, dose_proj, dose_sq):
+        out_ref[x, 256:320, :] = dproj_ref[0:64, 256 * x : 256 * x + 128]
+        out_ref[x, 320:384, :] = dproj_ref[0:64, 256 * x + 128 : 256 * x + 256]
+        dose_own = []
+        for z in range(8):
+            first = 256 * x + LANES * (z // 4)
+            row = dproj_ref[64:65, first : first + LANES]
+            dose_own.append(pltpu.roll(row, 96 - 32 * (z % 4), 1) if z % 4 < 3 else row)
+        pieces = jnp.concatenate(own + dose_own + [jnp.zeros((53, LANES), F32)], axis=0)
+        out_ref[x, 384:448, :] = jnp.where(spare, pieces, proj)
+
+
+def cross_products(bin_ids, table, dosages, covariates, plates, dose_proj):
     count, width = dosages.shape
     chunk = CROSS_CHUNK
     steps = width // chunk
@@ -362,9 +364,9 @@
     hbm = pl.BlockSpec(memory_space=pl.ANY)
     return pl.pallas_call(
         cross_kernel,
-        in_specs=[hbm, whole, hbm, hbm, hbm, whole, whole],
+        in_specs=[hbm, whole, hbm, hbm, hbm, whole],
         out_specs=whole,
-        out_shape=jax.ShapeDtypeStruct((4, 456, LANES), F32),
+        out_shape=jax.ShapeDtypeStruct((4, 448, LANES), F32),
         scratch_shapes=[
             pltpu.VMEM((steps, bin_ids.shape[0], chunk), jnp.int32),
             pltpu.VMEM((COVARS, width), F32),
@@ -376,22 +378,23 @@
             pltpu.VMEM((LANES, LANES), F32),
             pltpu.SemaphoreType.DMA((2 * steps + 2,)),
         ],
-        compiler_params=vmem_params(60),
+        compiler_params=vmem_params(50),
         name="cross_products",
-    )(bin_ids, table, dosages, covariates, plates, dose_proj, dose_sq)
+    )(bin_ids, table, dosages, covariates, plates, dose_proj)
 
 
 def regroup_kernel(parts_ref, out_ref):
     total = parts_ref[0] + parts_ref[1] + parts_ref[2] + parts_ref[3]
-    row = lax.broadcasted_iota(jnp.int32, (8, LANES), 0)
+    proj = total[384:448]
     for z in range(8):
-        out_ref[z, 0:32, :] = total[32 * z : 32 * z + 32]
-        out_ref[z, 32:48, :] = total[256 + 16 * z : 256 + 16 * z + 16]
-        out_ref[z, 48:112, :] = total[384:448]
-        squares = total[448:456]
-        own = squares[2 + z // 4 : 3 + z // 4]
-        own = pltpu.roll(own, (4 - z % 4) % 4 * 32, 1) if z % 4 else own
-        out_ref[z, 112:120, :] = jnp.where(row == 1, own, squares)
+        squares = jnp.concatenate(
+            [proj[0:3], proj[3 + z : 4 + z], jnp.zeros((28, LANES), F32)], axis=0
+        )
+        cross = total[32 * z : 32 * z + 32]
+        out_ref[z, 0:32, :] = jnp.where(lane_ids((32, LANES)) >= 96, squares, cross)
+        dose = total[256 + 64 * (z // 4) : 320 + 64 * (z // 4)]
+        dose = pltpu.roll(dose, 96 - 32 * (z % 4), 1) if z % 4 < 3 else dose
+        out_ref[z, 32:96, :] = jnp.where(lane_ids((64, LANES)) >= 96, dose, proj)
 
 
 def regroup(parts):
@@ -400,32 +403,76 @@
         regroup_kernel,
         in_specs=[whole],
         out_specs=whole,
-        out_shape=jax.ShapeDtypeStruct((8, 120, LANES), F32),
-        compiler_params=vmem_params(16),
+        out_shape=jax.ShapeDtypeStruct((8, 96, LANES), F32),
+        compiler_params=vmem_params(8),
         name="regroup",
     )(parts)
+
+
+def inverse_kernel(gram_ref, out_ref):
+    packed = gram_ref[...]
+    lane = lane_ids((DESIGN, LANES))
+    row = lax.broadcasted_iota(jnp.int32, (DESIGN, LANES), 0)
+    work = jnp.concatenate([packed, pltpu.roll(packed, 64, 1)], axis=0)
+    work = jnp.where(lane < DESIGN, work, jnp.where(lane == row + DESIGN, 1.0, 0.0))
+    plate = work[COVARS:]
+    low_lane = lane_ids((PLATES, LANES))
+    low_row = lax.broadcasted_iota(jnp.int32, (PLATES, LANES), 0)
+    pivots = jnp.sum(
+        jnp.where(low_lane == low_row + COVARS, plate, 0.0), axis=1, keepdims=True
+    )
+    upper = work[:COVARS]
+    coupling = upper[:, COVARS:DESIGN]
+    upper = upper - lax.dot_general(
+        coupling, plate * (1.0 / pivots), NN, precision=exact_mode, preferred_element_type=F32
+    )
+    for k in range(COVARS):
+        first = k // 8 * 8
+        source = upper[k : k + 1]
+        rest = upper[first:]
+        scale = 1.0 / source[:, k : k + 1]
+        below = lax.broadcasted_iota(jnp.int32, rest.shape, 0) > k - first
+        factor = jnp.where(below, rest[:, k : k + 1] * (source * scale), 0.0)
+        rest = rest - factor
+        upper = jnp.concatenate([upper[:first], rest], axis=0) if first else rest
+    work = jnp.concatenate([upper, plate], axis=0)
+    diagonal = jnp.sum(jnp.where(lane == row, work, 0.0), axis=1, keepdims=True)
+    out_ref[...] = pltpu.roll(work * lax.rsqrt(diagonal), 64, 1)[:, :DESIGN]
+
+
+def inverse_factor(table):
+    return pl.pallas_call(
+        inverse_kernel,
+        grid=(1,),
+        in_specs=[pl.BlockSpec((32, LANES), lambda i: (23, 0))],
+        out_specs=pl.BlockSpec((DESIGN, DESIGN), lambda i: (0, 0)),
+        out_shape=jax.ShapeDtypeStruct((DESIGN, DESIGN), F32),
+        compiler_params=vmem_params(8),
+        cost_estimate=pl.CostEstimate(flops=4_000_000_000, bytes_accessed=32768, transcendentals=0),
+        name="inverse_factor",
+    )(table)
 
 
 def finish_kernel(freedom, parts_ref, inverse_ref, out_ref):
     total = parts_ref[0]
     for z in range(1, 8):
         total = total + parts_ref[z]
-    cross, dose, proj, squares = total[0:32], total[32:48], total[48:112], total[112:113]
     shape = (32, LANES)
-    diagonal = lax.broadcasted_iota(jnp.int32, shape, 0) == lane_ids(shape)
-    dose_squares = jnp.sum(
-        jnp.where(diagonal, jnp.broadcast_to(total[113:114], shape), 0.0), axis=1, keepdims=True
-    )
-    inverse = inverse_ref[...]
-    dot = functools.partial(
-        lax.dot_general, precision=exact_mode, preferred_element_type=F32
-    )
-    expr_white = dot(inverse, proj, NN)
-    dose_both = jnp.concatenate([dose[:, :64], dose[:, 64:]], axis=0)
-    dose_white = dot(dose_both, inverse, NT)
-    expr_norm = squares - jnp.sum(expr_white * expr_white, axis=0, keepdims=True)
-    dose_norm = dose_squares - jnp.sum(dose_white * dose_white, axis=1, keepdims=True)
-    cross = cross - dot(dose_white, expr_white, NN)
+    lane = lane_ids((1, LANES))
+    white = lax.dot_general(
+        inverse_ref[...], total[32:96], NN, precision=exact_mode, preferred_element_type=F32
+    )
+    shared = lax.dot_general(
+        white, white, (((0,), (0,)), ((), ())), precision=exact_mode, preferred_element_type=F32
+    )
+    removed = jnp.sum(white * white, axis=0, keepdims=True)
+    expr_sq = [pltpu.roll(total[j : j + 1], 32 * j + 32, 1) for j in range(3)]
+    expr_sq = jnp.where(lane < 32, expr_sq[0], jnp.where(lane < 64, expr_sq[1], expr_sq[2]))
+    expr_norm = expr_sq - removed
+    own = lane_ids(shape) == lax.broadcasted_iota(jnp.int32, shape, 0) + 96
+    dose_norm = jnp.broadcast_to(total[3:4] - removed, shape)
+    dose_norm = jnp.sum(jnp.where(own, dose_norm, 0.0), axis=1, keepdims=True)
+    cross = total[0:32] - shared[96:128]
     corr = cross * lax.rsqrt(dose_norm * expr_norm + tiny_eps)
     stats = corr * jnp.sqrt(freedom / (1.0 - corr * corr))
     out_ref[...] = stats[:, : out_ref.shape[1]]
@@ -438,7 +485,7 @@
         in_specs=[whole, whole],
         out_specs=whole,
         out_shape=jax.ShapeDtypeStruct((32, proteins), F32),
-        compiler_params=vmem_params(16),
+        compiler_params=vmem_params(8),
         name="finish",
     )(parts, inverse)
 
@@ -452,19 +499,15 @@
 
     counts = histogram(bin_ids, covariates, plates).reshape(32, 24, LANES)
     counts = lax.all_to_all(counts, "samp", 0, 0, tiled=True)
-    dose_proj, dose_sq = dose_products(dosages, covariates, plates)
-    counts, dose_proj, dose_sq = lax.optimization_barrier((counts, dose_proj, dose_sq))
+    dose_proj = dose_products(dosages, covariates, plates)
+    counts, dose_proj = lax.optimization_barrier((counts, dose_proj))
     table = rank_table(counts, sample_total, base)
     table = lax.all_to_all(table, "samp", 0, 0, tiled=True).reshape(768, LANES)
-    parts = cross_products(bin_ids, table, dosages, covariates, plates, dose_proj, dose_sq)
-    packed, parts = lax.optimization_barrier((table[736:], parts))
-    gram = jnp.concatenate([packed[:, :64], packed[:, 64:]], axis=0)
-    factor = lax.linalg.cholesky(gram, symmetrize_input=False)
+    parts = cross_products(bin_ids, table, dosages, covariates, plates, dose_proj)
+    late_table, parts = lax.optimization_barrier((table, parts))
+    inverse = inverse_factor(late_table)
     parts = lax.all_to_all(parts, "samp", 0, 0, axis_index_groups=x_groups, tiled=True)
-    parts, factor = lax.optimization_barrier((parts, factor))
-    inverse = lax.linalg.triangular_solve(
-        factor, jnp.eye(DESIGN, dtype=F32), left_side=True, lower=True
-    )
+    parts, inverse = lax.optimization_barrier((parts, inverse))
     parts = regroup(parts)
     parts = lax.all_to_all(parts, "samp", 0, 0, axis_index_groups=z_groups, tiled=True)
     return finish(parts, inverse, sample_total - DESIGN - 1.0, bin_ids.shape[0])

time: 97.7 us -> 92.7 us (0.949)
  blocking collectives: 18.9 us -> 36.2 us
  other arithmetic: 12.1 us -> 0 us
  starting transfers between devices: 22.3 us -> 16.5 us
  waiting for transfers between devices: 17 us -> 11.9 us
  local copies, waits for them, and re-layouts: 0.82 us -> 1.81 us
    all_to_all x0 -> x1, blocking collectives: none -> 17.3 us  [body(): lax.all_to_all(parts, 'samp', 0, 0, axis_index_groups=z_groups, tiled=True)]
    another operation x5 -> x0, other arithmetic: 11.4 us -> none  [the longest x3 6.52 us: body(): factor = lax.linalg.cholesky(gram, symmetrize_input=False)]
    all_to_all x1 -> x0, waiting for transfers between devices: 8.53 us -> none  [body(): lax.all_to_all(parts, 'samp', 0, 0, axis_index_groups=z_groups, tiled=True)]
    all_to_all x1 -> x0, starting transfers between devices: 5.84 us -> none  [body(): lax.all_to_all(parts, 'samp', 0, 0, axis_index_groups=z_groups, tiled=True)]
    all_to_all x1, waiting for transfers between devices: 1.56 us -> 5.09 us  [body(): lax.all_to_all(parts, 'samp', 0, 0, axis_index_groups=x_groups, tiled=True)]
    pallas_call x1 -> x2, Pallas kernels: 9.43 us -> 11.7 us  [the longest x1 8.04 us: cross_products(): pl.pallas_call(cross_kernel, in_specs=[hbm, whole, hbm, hbm, hbm, whole],...]
    pallas_call x1, Pallas kernels: 6.41 us -> 4.71 us  [dose_products(): pl.pallas_call(dose_kernel, in_specs=[pl.BlockSpec(memory_space=pl.ANY),...]
    unnamed x2 -> x10, local copies, waits for them, and re-layouts: 0.75 us -> 1.81 us
  transfers between devices with their start and end apart: 3 -> 2, of which waited for: 3 -> 2; matrix products, arithmetic and copies ran while one was open for 13% -> 0% of each run, Pallas kernels for 7% -> 9%
where the time goes in v3:
time: 92.7 us; the launch traced here: 91.4 us
  blocking collectives  36.2 us (39%)
  Pallas kernels  24.9 us (27%)
  starting transfers between devices  16.5 us (18%)
  waiting for transfers between devices  11.9 us (13%)
  local copies, waits for them, and re-layouts  1.81 us (2%)
    all_to_all x1, blocking collectives, body(): table = lax.all_to_all(table, 'samp', 0, 0, tiled=True).reshape(768, LANES)  18.9 us
    all_to_all x1, blocking collectives, body(): lax.all_to_all(parts, 'samp', 0, 0, axis_index_groups=z_groups, tiled=True)  17.3 us
    all_to_all x1, starting transfers between devices, body(): counts = lax.all_to_all(counts, 'samp', 0, 0, tiled=True)  11.6 us
    pallas_call x1, Pallas kernels, cross_products(): pl.pallas_call(cross_kernel, in_specs=[hbm, whole, hbm, hbm, hbm, whole],...  8.04 us
    pallas_call x1, Pallas kernels, histogram(): pl.pallas_call(hist_kernel, in_specs=[hbm, hbm, hbm], out_specs=pl.BlockS...  6.91 us
    all_to_all x1, waiting for transfers between devices, body(): counts = lax.all_to_all(counts, 'samp', 0, 0, tiled=True)  6.81 us
    all_to_all x1, waiting for transfers between devices, body(): lax.all_to_all(parts, 'samp', 0, 0, axis_index_groups=x_groups, tiled=True)  5.09 us
    all_to_all x1, starting transfers between devices, body(): lax.all_to_all(parts, 'samp', 0, 0, axis_index_groups=x_groups, tiled=True)  4.89 us
  transfers between devices with their start and end apart: 2, of which 2 were waited for; matrix products, arithmetic and copies ran while one was open for 0% of the time, Pallas kernels for 9%

profile of v3, /device:TPU:26, one launch (start us, length us, event | category | flops | bytes accessed | tf_op | source)
XLA Modules:
  0.0 91.4 jit_solution(18101379879339889237)
XLA Ops:
  0.0 0.0 copy-start.4
  0.0 0.0 copy-start
  0.0 0.0 copy-start.2
  0.0 6.9 %histogram.1 = f32[768,128]{1,0:T(8,128)} custom-call(s32[92,4096]{1,0:T(8,128)} %bins_hbm.3, f32[40,4096]{1,0:T(8,128)} %cov_hbm.3, s32[1,4096]{1,0:T(1,128)} %bitcast.6), custom_call_target="tpu_custom_call" | custom-call | tf_op jit(solution)/shard_map/histogram/pallas_call | solution.py:117
  6.9 11.6 %all-to-all-start = ((f32[32,24,128]{2,1,0:T(8,128)}), f32[32,24,128]{2,1,0:T(8,128)S(1)}, u32[]{:S(2)}, u32[]{:S(2)}) async-start(f32[32,24,128]{2,1,0:T(8,128)} %bitcast.9), calls=%async_computation | async-start | bytes 786432 | tf_op jit(solution)/shard_map/all_to_all | solution.py:501
  18.6 0.0 copy-start.1
  18.6 1.1 %copy-done.1 = f32[40,4096]{1,0:T(8,128)S(1)} copy-done((f32[40,4096]{1,0:T(8,128)S(1)}, f32[40,4096]{1,0:T(8,128)}, u32[]{:S(2)}) %copy-start.1) | copy-done | bytes 655384
  19.7 0.0 copy-start.3
  19.7 0.7 copy-done.3
  20.4 4.7 %dose_products.1.dproj_ref = f32[72,1024]{1,0:T(8,128)S(1)} custom-call(bf16[1024,4096]{1,0:T(8,128)(2,1)} %dose_hbm.3, f32[40,4096]{1,0:T(8,128)S(1)} %copy-done.1, s32[1,4096]{1,0:T(1,128)S(1)} %bitcast.7), custom_call_target="tpu_custom_call" | custom-call | flops 2147483648 | bytes 8388608 | tf_op jit(solution)/shard_map/dose_products/pallas_call | solution.py:178
  25.1 6.8 %all-to-all-done.parts_ref = f32[32,24,128]{2,1,0:T(8,128)S(1)} async-done(((f32[32,24,128]{2,1,0:T(8,128)}), f32[32,24,128]{2,1,0:T(8,128)S(1)}, u32[]{:S(2)}, u32[]{:S(2)}) %all-to-all-start) | async-done | bytes 393248 | tf_op jit(solution)/shard_map/all_to_all | solution.py:501
  31.9 0.4 rank_table.1
  32.3 18.9 %all_to_all.20 = f32[32,24,128]{2,1,0:T(8,128)S(1)} all-to-all(f32[32,24,128]{2,1,0:T(8,128)S(1)} %rank_table.1), channel_id=1, replica_groups=mesh['samp'=32,'prot'=8] {'samp'}, dimensions={0} | all-to-all | bytes 786432 | tf_op jit(solution)/shard_map/all_to_all | solution.py:505
  51.1 0.0 copy-done.4
  51.1 0.0 copy-done
  51.2 0.0 copy-done.2
  51.2 8.0 %cross_products.1 = f32[4,448,128]{2,1,0:T(8,128)} custom-call(s32[92,4096]{1,0:T(8,128)S(1)} %copy-done, f32[768,128]{1,0:T(8,128)S(1)} %bitcast.4, bf16[1024,4096]{1,0:T(8,128)(2,1)} %dose_hbm.3, f32[40,4096]{1,0:T(8,128)S(1)} %copy-done.2, s32[1,4096]{1,0:T(1,128)S(1)} %bitcast.8, f32[72,1024]{1,0:T(8,128)S(1)} %dose_products.1.dproj_ref), custom_call_target="tpu_custom_call" | custom-call | tf_op jit(solution)/shard_map/cross_products/pallas_call | solution.py:365
  59.2 4.9 %all-to-all-start.2 = ((f32[4,448,128]{2,1,0:T(8,128)}), f32[4,448,128]{2,1,0:T(8,128)S(1)}, u32[]{:S(2)}, u32[]{:S(2)}) async-start(f32[4,448,128]{2,1,0:T(8,128)} %cross_products.1), calls=%async_computation.2 | async-start | bytes 1835008 | tf_op jit(solution)/shard_map/all_to_all | solution.py:509
  64.1 3.6 %inverse_factor.1.inverse_ref = f32[64,64]{1,0:T(8,128)S(1)} custom-call(f32[768,128]{1,0:T(8,128)S(1)} %bitcast.5), custom_call_target="tpu_custom_call" | custom-call | flops 4000000000 | bytes 32768 | tf_op jit(solution)/shard_map/inverse_factor/pallas_call | solution.py:444
  67.7 5.1 %all-to-all-done.2.parts_ref = f32[4,448,128]{2,1,0:T(8,128)S(1)} async-done(((f32[4,448,128]{2,1,0:T(8,128)}), f32[4,448,128]{2,1,0:T(8,128)S(1)}, u32[]{:S(2)}, u32[]{:S(2)}) %all-to-all-start.2) | async-done | bytes 917536 | tf_op jit(solution)/shard_map/all_to_all | solution.py:509
  72.8 0.1 regroup.1
  73.0 17.3 %all_to_all.21.parts_ref = f32[8,96,128]{2,1,0:T(8,128)S(1)} all-to-all(f32[8,96,128]{2,1,0:T(8,128)S(1)} %regroup.1), channel_id=1, replica_groups={{0,8,16,24,32,40,48,56},{64,72,80,88,96,104,112,120},{128,136,144,152,1..., dimensions={0} | all-to-all | bytes 786432 | tf_op jit(solution)/shard_map/all_to_all | solution.py:512
  90.3 1.1 %finish.1 = f32[32,92]{1,0:T(8,128)} custom-call(f32[8,96,128]{2,1,0:T(8,128)S(1)} %all_to_all.21.parts_ref, f32[64,64]{1,0:T(8,128)S(1)} %inverse_factor.1.inverse_ref), custom_call_target="tpu_custom_call" | custom-call | tf_op jit(solution)/shard_map/finish/pallas_call | solution.py:483
Async XLA Ops:
  0.0 51.1 %copy-start.4 = (s32[4096]{0:T(1024)S(1)}, s32[4096]{0:T(1024)}, u32[]{:S(2)}) copy-start(s32[4096]{0:T(1024)} %param.5) | copy-start | bytes 49156
  0.0 51.1 %copy-start = (s32[92,4096]{1,0:T(8,128)S(1)}, s32[92,4096]{1,0:T(8,128)}, u32[]{:S(2)}) copy-start(s32[92,4096]{1,0:T(8,128)} %bins_hbm.3) | copy-start | bytes 4521988
  0.0 51.1 %copy-start.2 = (f32[40,4096]{1,0:T(8,128)S(1)}, f32[40,4096]{1,0:T(8,128)}, u32[]{:S(2)}) copy-start(f32[40,4096]{1,0:T(8,128)} %cov_hbm.3) | copy-start | bytes 1966084
  6.9 25.0 %all-to-all-start = ((f32[32,24,128]{2,1,0:T(8,128)}), f32[32,24,128]{2,1,0:T(8,128)S(1)}, u32[]{:S(2)}, u32[]{:S(2)}) async-start(f32[32,24,128]{2,1,0:T(8,128)} %bitcast.9), calls=%async_computation | async-start | bytes 786432 | tf_op jit(solution)/shard_map/all_to_all | solution.py:501
  18.6 1.1 %copy-start.1 = (f32[40,4096]{1,0:T(8,128)S(1)}, f32[40,4096]{1,0:T(8,128)}, u32[]{:S(2)}) copy-start(f32[40,4096]{1,0:T(8,128)} %cov_hbm.3) | copy-start | bytes 1966084
  19.7 0.7 copy-start.3
  59.2 13.6 %all-to-all-start.2 = ((f32[4,448,128]{2,1,0:T(8,128)}), f32[4,448,128]{2,1,0:T(8,128)S(1)}, u32[]{:S(2)}, u32[]{:S(2)}) async-start(f32[4,448,128]{2,1,0:T(8,128)} %cross_products.1), calls=%async_computation.2 | async-start | bytes 1835008 | tf_op jit(solution)/shard_map/all_to_all | solution.py:509

commit v4 on v3

--- a/solution.py
+++ b/solution.py
@@ -262,8 +262,8 @@
 
 
 def cross_kernel(
-    bins_hbm, table_ref, dose_hbm, cov_hbm, plate_hbm, dproj_ref,
-    out_ref, bins_ref, cov_ref, plate_ref, dose_ref, level_ref, total_ref, design_ref, square_ref, sems,
+    place_ref, bins_hbm, table_ref, dose_hbm, cov_hbm, plate_hbm, dproj_ref,
+    out0_ref, out1_ref, out2_ref, out3_ref, bins_ref, cov_ref, plate_ref, dose_ref, level_ref, total_ref, design_ref, square_ref, sems,
 ):
     proteins, width = bins_hbm.shape
     chunk = dose_ref.shape[2]
@@ -342,21 +342,25 @@
     )
     spare = lane_ids((64, LANES)) >= 96
     own = [pltpu.roll(squares[0:1], shift, 1) for shift in (96, 64, 32)]
-    for x in range(4):
-        rows = slice(256 * x, 256 * x + 256)
-        out_ref[x, 0:256, :] = total_ref[rows, :LANES] + total_ref[rows, LANES:]
-        out_ref[x, 256:320, :] = dproj_ref[0:64, 256 * x : 256 * x + 128]
-        out_ref[x, 320:384, :] = dproj_ref[0:64, 256 * x + 128 : 256 * x + 256]
+    for d, out_ref in enumerate((out0_ref, out1_ref, out2_ref, out3_ref)):
+        x = lax.rem(place_ref[1] + d, 4)
+        first = pl.multiple_of(256 * x, 256)
+        second = pl.multiple_of(256 * x + LANES, LANES)
+        rows = total_ref[pl.ds(first, 256), :]
+        out_ref[0:256, :] = rows[:, :LANES] + rows[:, LANES:]
+        low = dproj_ref[:, pl.ds(first, LANES)]
+        high = dproj_ref[:, pl.ds(second, LANES)]
+        out_ref[256:320, :] = low[0:64]
+        out_ref[320:384, :] = high[0:64]
         dose_own = []
         for z in range(8):
-            first = 256 * x + LANES * (z // 4)
-            row = dproj_ref[64:65, first : first + LANES]
+            row = (low, high)[z // 4][64:65]
             dose_own.append(pltpu.roll(row, 96 - 32 * (z % 4), 1) if z % 4 < 3 else row)
         pieces = jnp.concatenate(own + dose_own + [jnp.zeros((53, LANES), F32)], axis=0)
-        out_ref[x, 384:448, :] = jnp.where(spare, pieces, proj)
-
-
-def cross_products(bin_ids, table, dosages, covariates, plates, dose_proj):
+        out_ref[384:448, :] = jnp.where(spare, pieces, proj)
+
+
+def cross_products(place, bin_ids, table, dosages, covariates, plates, dose_proj):
     count, width = dosages.shape
     chunk = CROSS_CHUNK
     steps = width // chunk
@@ -364,9 +368,9 @@
     hbm = pl.BlockSpec(memory_space=pl.ANY)
     return pl.pallas_call(
         cross_kernel,
-        in_specs=[hbm, whole, hbm, hbm, hbm, whole],
-        out_specs=whole,
-        out_shape=jax.ShapeDtypeStruct((4, 448, LANES), F32),
+        in_specs=[pl.BlockSpec(memory_space=pltpu.SMEM), hbm, whole, hbm, hbm, hbm, whole],
+        out_specs=[whole] * 4,
+        out_shape=[jax.ShapeDtypeStruct((448, LANES), F32)] * 4,
         scratch_shapes=[
             pltpu.VMEM((steps, bin_ids.shape[0], chunk), jnp.int32),
             pltpu.VMEM((COVARS, width), F32),
@@ -380,11 +384,11 @@
         ],
         compiler_params=vmem_params(50),
         name="cross_products",
-    )(bin_ids, table, dosages, covariates, plates, dose_proj)
-
-
-def regroup_kernel(parts_ref, out_ref):
-    total = parts_ref[0] + parts_ref[1] + parts_ref[2] + parts_ref[3]
+    )(place, bin_ids, table, dosages, covariates, plates, dose_proj)
+
+
+def regroup_kernel(own_ref, first_ref, second_ref, third_ref, out_ref):
+    total = own_ref[...] + first_ref[...] + second_ref[...] + third_ref[...]
     proj = total[384:448]
     for z in range(8):
         squares = jnp.concatenate(
@@ -397,16 +401,16 @@
         out_ref[z, 32:96, :] = jnp.where(lane_ids((64, LANES)) >= 96, dose, proj)
 
 
-def regroup(parts):
+def regroup(*parts):
     whole = pl.BlockSpec(memory_space=pltpu.VMEM)
     return pl.pallas_call(
         regroup_kernel,
-        in_specs=[whole],
+        in_specs=[whole] * 4,
         out_specs=whole,
         out_shape=jax.ShapeDtypeStruct((8, 96, LANES), F32),
         compiler_params=vmem_params(8),
         name="regroup",
-    )(parts)
+    )(*parts)
 
 
 def inverse_kernel(gram_ref, out_ref):
@@ -493,9 +497,9 @@
 def body(bin_ids, plate_ids, covariates, dosages):
     sample_total = bin_ids.shape[1] * lax.axis_size("samp")
     plates = plate_ids[None, :]
-    x_groups = [[x * 8 + z for x in range(4)] for z in range(8)]
     z_groups = [[x * 8 + z for z in range(8)] for x in range(4)]
-    base = (lax.axis_index("samp") * 24).astype(jnp.int32)[None]
+    me = lax.axis_index("samp").astype(jnp.int32)
+    base = jnp.stack([me * 24, me // 8])
 
     counts = histogram(bin_ids, covariates, plates).reshape(32, 24, LANES)
     counts = lax.all_to_all(counts, "samp", 0, 0, tiled=True)
@@ -503,12 +507,17 @@
     counts, dose_proj = lax.optimization_barrier((counts, dose_proj))
     table = rank_table(counts, sample_total, base)
     table = lax.all_to_all(table, "samp", 0, 0, tiled=True).reshape(768, LANES)
-    parts = cross_products(bin_ids, table, dosages, covariates, plates, dose_proj)
-    late_table, parts = lax.optimization_barrier((table, parts))
+    own, *others = cross_products(
+        base, bin_ids, table, dosages, covariates, plates, dose_proj
+    )
+    late_table, own = lax.optimization_barrier((table, own))
     inverse = inverse_factor(late_table)
-    parts = lax.all_to_all(parts, "samp", 0, 0, axis_index_groups=x_groups, tiled=True)
-    parts, inverse = lax.optimization_barrier((parts, inverse))
-    parts = regroup(parts)
+    moved = {}
+    for d in (2, 1, 3):
+        pairs = [(x * 8 + z, (x + d) % 4 * 8 + z) for x in range(4) for z in range(8)]
+        moved[d] = lax.ppermute(others[d - 1], "samp", pairs)
+    own, inverse = lax.optimization_barrier((own, inverse))
+    parts = regroup(own, moved[1], moved[2], moved[3])
     parts = lax.all_to_all(parts, "samp", 0, 0, axis_index_groups=z_groups, tiled=True)
     return finish(parts, inverse, sample_total - DESIGN - 1.0, bin_ids.shape[0])
 

time: 92.7 us -> 91.7 us (0.989); the launches traced: 91.4 us -> 91.3 us
  blocking collectives: 36.2 us -> 38 us
  waiting for transfers between devices: 11.9 us -> 10.2 us
    all_to_all x1 -> x0, waiting for transfers between devices: 5.09 us -> none  [body(): lax.all_to_all(parts, 'samp', 0, 0, axis_index_groups=x_groups, tiled=True)]
    all_to_all x1 -> x0, starting transfers between devices: 4.89 us -> none  [body(): lax.all_to_all(parts, 'samp', 0, 0, axis_index_groups=x_groups, tiled=True)]
    ppermute x0 -> x3, starting transfers between devices: none -> 4.3 us  [body(): moved[d] = lax.ppermute(others[d - 1], 'samp', pairs)]
    ppermute x0 -> x3, waiting for transfers between devices: none -> 3.51 us  [body(): moved[d] = lax.ppermute(others[d - 1], 'samp', pairs)]
    all_to_all x1, blocking collectives: 17.3 us -> 19.1 us  [body(): lax.all_to_all(parts, 'samp', 0, 0, axis_index_groups=z_groups, tiled=True)]
  transfers between devices with their start and end apart: 2 -> 4, of which waited for: 2 -> 3; matrix products, arithmetic and copies ran while one was open for 0% -> 0% of each run, Pallas kernels for 9% -> 9%
where the time goes in v4:
time: 91.7 us; the launch traced here: 91.3 us
  blocking collectives  38 us (41%)
  Pallas kernels  25.2 us (27%)
  starting transfers between devices  15.9 us (17%)
  waiting for transfers between devices  10.2 us (11%)
  local copies, waits for them, and re-layouts  1.82 us (2%)
    all_to_all x1, blocking collectives, body(): lax.all_to_all(parts, 'samp', 0, 0, axis_index_groups=z_groups, tiled=True)  19.1 us
    all_to_all x1, blocking collectives, body(): table = lax.all_to_all(table, 'samp', 0, 0, tiled=True).reshape(768, LANES)  18.9 us
    all_to_all x1, starting transfers between devices, body(): counts = lax.all_to_all(counts, 'samp', 0, 0, tiled=True)  11.6 us
    pallas_call x1, Pallas kernels, cross_products(): pl.pallas_call(cross_kernel, in_specs=[pl.BlockSpec(memory_space=pltpu.SM...  7.77 us
    pallas_call x1, Pallas kernels, histogram(): pl.pallas_call(hist_kernel, in_specs=[hbm, hbm, hbm], out_specs=pl.BlockS...  6.92 us
    all_to_all x1, waiting for transfers between devices, body(): counts = lax.all_to_all(counts, 'samp', 0, 0, tiled=True)  6.73 us
    pallas_call x1, Pallas kernels, dose_products(): pl.pallas_call(dose_kernel, in_specs=[pl.BlockSpec(memory_space=pl.ANY),...  4.7 us
    ppermute x3, starting transfers between devices, body(): moved[d] = lax.ppermute(others[d - 1], 'samp', pairs)  4.3 us
  transfers between devices with their start and end apart: 4, of which 3 were waited for; matrix products, arithmetic and copies ran while one was open for 0% of the time, Pallas kernels for 9%

profile of v4, /device:TPU:26, one launch (start us, length us, event | category | flops | bytes accessed | tf_op | source)
XLA Modules:
  0.0 91.3 jit_solution(12543419783481136774)
XLA Ops:
  0.0 0.0 copy-start.2
  0.0 0.0 copy-start
  0.0 0.0 copy-start.4
  0.0 6.9 %histogram.1 = f32[768,128]{1,0:T(8,128)} custom-call(s32[92,4096]{1,0:T(8,128)} %bins_hbm.3, f32[40,4096]{1,0:T(8,128)} %cov_hbm.3, s32[1,4096]{1,0:T(1,128)} %bitcast.7), custom_call_target="tpu_custom_call" | custom-call | tf_op jit(solution)/shard_map/histogram/pallas_call | solution.py:117
  6.9 11.6 %all-to-all-start = ((f32[32,24,128]{2,1,0:T(8,128)}), f32[32,24,128]{2,1,0:T(8,128)S(1)}, u32[]{:S(2)}, u32[]{:S(2)}) async-start(f32[32,24,128]{2,1,0:T(8,128)} %bitcast.10), calls=%async_computation | async-start | bytes 786432 | tf_op jit(solution)/shard_map/all_to_all | solution.py:505
  18.6 0.1 pad_add_fusion.base_ref.place_ref
  18.7 0.0 copy-start.1
  18.7 1.1 %copy-done.1 = f32[40,4096]{1,0:T(8,128)S(1)} copy-done((f32[40,4096]{1,0:T(8,128)S(1)}, f32[40,4096]{1,0:T(8,128)}, u32[]{:S(2)}) %copy-start.1) | copy-done | bytes 655384
  19.8 0.0 copy-start.3
  19.8 0.7 copy-done.3
  20.5 4.7 %dose_products.1.dproj_ref = f32[72,1024]{1,0:T(8,128)S(1)} custom-call(bf16[1024,4096]{1,0:T(8,128)(2,1)} %dose_hbm.3, f32[40,4096]{1,0:T(8,128)S(1)} %copy-done.1, s32[1,4096]{1,0:T(1,128)S(1)} %bitcast.8), custom_call_target="tpu_custom_call" | custom-call | flops 2147483648 | bytes 8388608 | tf_op jit(solution)/shard_map/dose_products/pallas_call | solution.py:178
  25.2 6.7 %all-to-all-done.parts_ref = f32[32,24,128]{2,1,0:T(8,128)S(1)} async-done(((f32[32,24,128]{2,1,0:T(8,128)}), f32[32,24,128]{2,1,0:T(8,128)S(1)}, u32[]{:S(2)}, u32[]{:S(2)}) %all-to-all-start) | async-done | bytes 393248 | tf_op jit(solution)/shard_map/all_to_all | solution.py:505
  31.9 0.9 %rank_table.1 = f32[32,24,128]{2,1,0:T(8,128)S(1)} custom-call(s32[2]{0:T(128)S(1)} %pad_add_fusion.base_ref.place_ref, f32[32,24,128]{2,1,0:T(8,128)S(1)} %all-to-all-done.parts_ref), custom_call_target="tpu_custom_call" | custom-call | tf_op jit(solution)/shard_map/rank_table/pallas_call | solution.py:240
  32.8 18.9 %all_to_all.15 = f32[32,24,128]{2,1,0:T(8,128)S(1)} all-to-all(f32[32,24,128]{2,1,0:T(8,128)S(1)} %rank_table.1), channel_id=1, replica_groups=mesh['samp'=32,'prot'=8] {'samp'}, dimensions={0} | all-to-all | bytes 786432 | tf_op jit(solution)/shard_map/all_to_all | solution.py:509
  51.7 0.0 copy-done.2
  51.7 0.0 copy-done
  51.7 0.0 copy-done.4
  51.7 7.8 %cross_products.1 = (f32[448,128]{1,0:T(8,128)S(1)}, f32[448,128]{1,0:T(8,128)S(1)}, f32[448,128]{1,0:T(8,128)S(1)}, f32[448,128]{1,0:T(8,128)S(1)}) custom-call(s32[2]{0:T(128)S(1)} %pad_add_fusion.base_ref.place_ref, s32[92,4096]{1,0:T(8,128)S(1)} %copy-done, f32[768,128]{1,0:T(8,128)S(1)} %bitcast.5, bf16[1024,4096]{1,0:T(8,128)(2,1)} %dose_hbm.3, ...), custom_call_target="tpu_custom_call" | custom-call | tf_op jit(solution)/shard_map/cross_products/pallas_call | solution.py:369
  59.5 1.2 %collective-permute-start = (f32[448,128]{1,0:T(8,128)S(1)}, f32[448,128]{1,0:T(8,128)S(1)}, u32[]{:S(2)}, u32[]{:S(2)}) collective-permute-start(f32[448,128]{1,0:T(8,128)S(1)} %get-tuple-element.21), channel_id=1, source_target_pairs={{0,64},{8,72},{16,80},{24,88},{32,96},{40,104},{48,112},{56,120},{... | collective-permute-start | bytes 688136 | tf_op jit(solution)/shard_map/ppermute | solution.py:518
  60.6 2.4 %collective-permute-start.1 = (f32[448,128]{1,0:T(8,128)S(1)}, f32[448,128]{1,0:T(8,128)S(1)}, u32[]{:S(2)}, u32[]{:S(2)}) collective-permute-start(f32[448,128]{1,0:T(8,128)S(1)} %get-tuple-element.22), channel_id=1, source_target_pairs={{0,128},{8,136},{16,144},{24,152},{32,160},{40,168},{48,176},{56,1... | collective-permute-start | bytes 688136 | tf_op jit(solution)/shard_map/ppermute | solution.py:518
  63.0 0.8 collective-permute-start.2
  63.8 3.6 %inverse_factor.1.inverse_ref = f32[64,64]{1,0:T(8,128)S(1)} custom-call(f32[768,128]{1,0:T(8,128)S(1)} %bitcast.6), custom_call_target="tpu_custom_call" | custom-call | flops 4000000000 | bytes 32768 | tf_op jit(solution)/shard_map/inverse_factor/pallas_call | solution.py:448
  67.4 0.0 collective-permute-done.first_ref
  67.4 1.2 %collective-permute-done.1.second_ref = f32[448,128]{1,0:T(8,128)S(1)} collective-permute-done((f32[448,128]{1,0:T(8,128)S(1)}, f32[448,128]{1,0:T(8,128)S(1)}, u32[]{:S(2)}, u32[]{:S(2)}) %collective-permute-start.1) | collective-permute-done | bytes 229408 | tf_op jit(solution)/shard_map/ppermute | solution.py:518
  68.6 2.4 %collective-permute-done.2.third_ref = f32[448,128]{1,0:T(8,128)S(1)} collective-permute-done((f32[448,128]{1,0:T(8,128)S(1)}, f32[448,128]{1,0:T(8,128)S(1)}, u32[]{:S(2)}, u32[]{:S(2)}) %collective-permute-start.2) | collective-permute-done | bytes 229408 | tf_op jit(solution)/shard_map/ppermute | solution.py:518
  70.9 0.1 regroup.1
  71.1 19.1 %all_to_all.16.parts_ref = f32[8,96,128]{2,1,0:T(8,128)S(1)} all-to-all(f32[8,96,128]{2,1,0:T(8,128)S(1)} %regroup.1), channel_id=1, replica_groups={{0,8,16,24,32,40,48,56},{64,72,80,88,96,104,112,120},{128,136,144,152,1..., dimensions={0} | all-to-all | bytes 786432 | tf_op jit(solution)/shard_map/all_to_all | solution.py:521
  90.2 1.1 %finish.1 = f32[32,92]{1,0:T(8,128)} custom-call(f32[8,96,128]{2,1,0:T(8,128)S(1)} %all_to_all.16.parts_ref, f32[64,64]{1,0:T(8,128)S(1)} %inverse_factor.1.inverse_ref), custom_call_target="tpu_custom_call" | custom-call | tf_op jit(solution)/shard_map/finish/pallas_call | solution.py:487
Async XLA Ops:
  0.0 51.7 %copy-start.2 = (f32[40,4096]{1,0:T(8,128)S(1)}, f32[40,4096]{1,0:T(8,128)}, u32[]{:S(2)}) copy-start(f32[40,4096]{1,0:T(8,128)} %cov_hbm.3) | copy-start | bytes 1966084
  0.0 51.7 %copy-start = (s32[92,4096]{1,0:T(8,128)S(1)}, s32[92,4096]{1,0:T(8,128)}, u32[]{:S(2)}) copy-start(s32[92,4096]{1,0:T(8,128)} %bins_hbm.3) | copy-start | bytes 4521988
  0.0 51.7 %copy-start.4 = (s32[4096]{0:T(1024)S(1)}, s32[4096]{0:T(1024)}, u32[]{:S(2)}) copy-start(s32[4096]{0:T(1024)} %param.5) | copy-start | bytes 49156
  6.9 25.0 %all-to-all-start = ((f32[32,24,128]{2,1,0:T(8,128)}), f32[32,24,128]{2,1,0:T(8,128)S(1)}, u32[]{:S(2)}, u32[]{:S(2)}) async-start(f32[32,24,128]{2,1,0:T(8,128)} %bitcast.10), calls=%async_computation | async-start | bytes 786432 | tf_op jit(solution)/shard_map/all_to_all | solution.py:505
  18.7 1.1 %copy-start.1 = (f32[40,4096]{1,0:T(8,128)S(1)}, f32[40,4096]{1,0:T(8,128)}, u32[]{:S(2)}) copy-start(f32[40,4096]{1,0:T(8,128)} %cov_hbm.3) | copy-start | bytes 1966084
  19.8 0.7 copy-start.3
  59.5 8.0 %collective-permute-start = (f32[448,128]{1,0:T(8,128)S(1)}, f32[448,128]{1,0:T(8,128)S(1)}, u32[]{:S(2)}, u32[]{:S(2)}) collective-permute-start(f32[448,128]{1,0:T(8,128)S(1)} %get-tuple-element.21), channel_id=1, source_target_pairs={{0,64},{8,72},{16,80},{24,88},{32,96},{40,104},{48,112},{56,120},{... | collective-permute-start | bytes 688136 | tf_op jit(solution)/shard_map/ppermute | solution.py:518
  60.6 7.9 %collective-permute-start.1 = (f32[448,128]{1,0:T(8,128)S(1)}, f32[448,128]{1,0:T(8,128)S(1)}, u32[]{:S(2)}, u32[]{:S(2)}) collective-permute-start(f32[448,128]{1,0:T(8,128)S(1)} %get-tuple-element.22), channel_id=1, source_target_pairs={{0,128},{8,136},{16,144},{24,152},{32,160},{40,168},{48,176},{56,1... | collective-permute-start | bytes 688136 | tf_op jit(solution)/shard_map/ppermute | solution.py:518
  63.0 7.9 %collective-permute-start.2 = (f32[448,128]{1,0:T(8,128)S(1)}, f32[448,128]{1,0:T(8,128)S(1)}, u32[]{:S(2)}, u32[]{:S(2)}) collective-permute-start(f32[448,128]{1,0:T(8,128)S(1)} %get-tuple-element.23), channel_id=1, source_target_pairs={{0,192},{8,200},{16,208},{24,216},{32,224},{40,232},{48,240},{56,2... | collective-permute-start | bytes 688136 | tf_op jit(solution)/shard_map/ppermute | solution.py:518

commit v5 on v4

--- a/solution.py
+++ b/solution.py
@@ -212,7 +212,7 @@
     return value * x
 
 
-def table_kernel(sample_total, base_ref, parts_ref, out_ref):
+def table_kernel(sample_total, parts_ref, out_ref):
     counts = jnp.sum(parts_ref[...], axis=0)
     rows = counts.shape[0]
     row = lax.broadcasted_iota(jnp.int32, (LANES, LANES), 0)
@@ -230,24 +230,21 @@
     middle = inside + outside + 0.5 * (counts + 1.0)
     level = (middle - 0.375) / (sample_total + 0.25)
     values = math.sqrt(2.0) * erf_inverse(2.0 * level - 1.0)
-    place = base_ref[0] + lax.broadcasted_iota(jnp.int32, counts.shape, 0)
+    place = lax.axis_index("samp") * rows + lax.broadcasted_iota(jnp.int32, counts.shape, 0)
     values = jnp.where(place < 736, values, counts)
     for n in range(out_ref.shape[0]):
         out_ref[n] = values
 
 
-def rank_table(parts, sample_total, base):
+def rank_table(parts, sample_total):
     return pl.pallas_call(
         functools.partial(table_kernel, float(sample_total)),
-        in_specs=[
-            pl.BlockSpec(memory_space=pltpu.SMEM),
-            pl.BlockSpec(memory_space=pltpu.VMEM),
-        ],
+        in_specs=[pl.BlockSpec(memory_space=pltpu.VMEM)],
         out_specs=pl.BlockSpec(memory_space=pltpu.VMEM),
         out_shape=jax.ShapeDtypeStruct(parts.shape, F32),
         compiler_params=vmem_params(8),
         name="rank_table",
-    )(base, parts)
+    )(parts)
 
 
 def lookup(bins, tables):
@@ -262,7 +259,7 @@
 
 
 def cross_kernel(
-    place_ref, bins_hbm, table_ref, dose_hbm, cov_hbm, plate_hbm, dproj_ref,
+    bins_hbm, table_ref, dose_hbm, cov_hbm, plate_hbm, dproj_ref,
     out0_ref, out1_ref, out2_ref, out3_ref, bins_ref, cov_ref, plate_ref, dose_ref, level_ref, total_ref, design_ref, square_ref, sems,
 ):
     proteins, width = bins_hbm.shape
@@ -343,7 +340,7 @@
     spare = lane_ids((64, LANES)) >= 96
     own = [pltpu.roll(squares[0:1], shift, 1) for shift in (96, 64, 32)]
     for d, out_ref in enumerate((out0_ref, out1_ref, out2_ref, out3_ref)):
-        x = lax.rem(place_ref[1] + d, 4)
+        x = lax.rem(lax.axis_index("samp") // 8 + d, 4)
         first = pl.multiple_of(256 * x, 256)
         second = pl.multiple_of(256 * x + LANES, LANES)
         rows = total_ref[pl.ds(first, 256), :]
@@ -360,7 +357,7 @@
         out_ref[384:448, :] = jnp.where(spare, pieces, proj)
 
 
-def cross_products(place, bin_ids, table, dosages, covariates, plates, dose_proj):
+def cross_products(bin_ids, table, dosages, covariates, plates, dose_proj):
     count, width = dosages.shape
     chunk = CROSS_CHUNK
     steps = width // chunk
@@ -368,7 +365,7 @@
     hbm = pl.BlockSpec(memory_space=pl.ANY)
     return pl.pallas_call(
         cross_kernel,
-        in_specs=[pl.BlockSpec(memory_space=pltpu.SMEM), hbm, whole, hbm, hbm, hbm, whole],
+        in_specs=[hbm, whole, hbm, hbm, hbm, whole],
         out_specs=[whole] * 4,
         out_shape=[jax.ShapeDtypeStruct((448, LANES), F32)] * 4,
         scratch_shapes=[
@@ -384,7 +381,7 @@
         ],
         compiler_params=vmem_params(50),
         name="cross_products",
-    )(place, bin_ids, table, dosages, covariates, plates, dose_proj)
+    )(bin_ids, table, dosages, covariates, plates, dose_proj)
 
 
 def regroup_kernel(own_ref, first_ref, second_ref, third_ref, out_ref):
@@ -498,17 +495,15 @@
     sample_total = bin_ids.shape[1] * lax.axis_size("samp")
     plates = plate_ids[None, :]
     z_groups = [[x * 8 + z for z in range(8)] for x in range(4)]
-    me = lax.axis_index("samp").astype(jnp.int32)
-    base = jnp.stack([me * 24, me // 8])
 
     counts = histogram(bin_ids, covariates, plates).reshape(32, 24, LANES)
     counts = lax.all_to_all(counts, "samp", 0, 0, tiled=True)
     dose_proj = dose_products(dosages, covariates, plates)
     counts, dose_proj = lax.optimization_barrier((counts, dose_proj))
-    table = rank_table(counts, sample_total, base)
+    table = rank_table(counts, sample_total)
     table = lax.all_to_all(table, "samp", 0, 0, tiled=True).reshape(768, LANES)
     own, *others = cross_products(
-        base, bin_ids, table, dosages, covariates, plates, dose_proj
+        bin_ids, table, dosages, covariates, plates, dose_proj
     )
     late_table, own = lax.optimization_barrier((table, own))
     inverse = inverse_factor(late_table)

time: 91.7 us -> 90.6 us (0.988)
  Pallas kernels: 25.2 us -> 24.1 us
where the time goes in v5:
time: 90.6 us; the launch traced here: 90.2 us
  blocking collectives  38 us (42%)
  Pallas kernels  24.1 us (27%)
  starting transfers between devices  15.9 us (18%)
  waiting for transfers between devices  10.3 us (11%)
  local copies, waits for them, and re-layouts  1.81 us (2%)
    all_to_all x1, blocking collectives, body(): lax.all_to_all(parts, 'samp', 0, 0, axis_index_groups=z_groups, tiled=True)  19.2 us
    all_to_all x1, blocking collectives, body(): table = lax.all_to_all(table, 'samp', 0, 0, tiled=True).reshape(768, LANES)  18.9 us
    all_to_all x1, starting transfers between devices, body(): counts = lax.all_to_all(counts, 'samp', 0, 0, tiled=True)  11.6 us
    pallas_call x1, Pallas kernels, cross_products(): pl.pallas_call(cross_kernel, in_specs=[hbm, whole, hbm, hbm, hbm, whole],...  7.22 us
    pallas_call x1, Pallas kernels, histogram(): pl.pallas_call(hist_kernel, in_specs=[hbm, hbm, hbm], out_specs=pl.BlockS...  6.92 us
    all_to_all x1, waiting for transfers between devices, body(): counts = lax.all_to_all(counts, 'samp', 0, 0, tiled=True)  6.82 us
    pallas_call x1, Pallas kernels, dose_products(): pl.pallas_call(dose_kernel, in_specs=[pl.BlockSpec(memory_space=pl.ANY),...  4.7 us
    ppermute x3, starting transfers between devices, body(): moved[d] = lax.ppermute(others[d - 1], 'samp', pairs)  4.3 us
  transfers between devices with their start and end apart: 4, of which 3 were waited for; matrix products, arithmetic and copies ran while one was open for 0% of the time, Pallas kernels for 9%

profile of v5, /device:TPU:26, one launch (start us, length us, event | category | flops | bytes accessed | tf_op | source)
XLA Modules:
  0.0 90.2 jit_solution(17375576360204980176)
XLA Ops:
  0.0 0.0 copy-start.2
  0.0 0.0 copy-start
  0.0 0.0 copy-start.4
  0.0 6.9 %histogram.1 = f32[768,128]{1,0:T(8,128)} custom-call(s32[92,4096]{1,0:T(8,128)} %bins_hbm.3, f32[40,4096]{1,0:T(8,128)} %cov_hbm.3, s32[1,4096]{1,0:T(1,128)} %bitcast.5), custom_call_target="tpu_custom_call" | custom-call | tf_op jit(solution)/shard_map/histogram/pallas_call | solution.py:117
  6.9 11.6 %all-to-all-start = ((f32[32,24,128]{2,1,0:T(8,128)}), f32[32,24,128]{2,1,0:T(8,128)S(1)}, u32[]{:S(2)}, u32[]{:S(2)}) async-start(f32[32,24,128]{2,1,0:T(8,128)} %bitcast.8), calls=%async_computation | async-start | bytes 786432 | tf_op jit(solution)/shard_map/all_to_all | solution.py:500
  18.6 0.0 copy-start.1
  18.6 1.1 %copy-done.1 = f32[40,4096]{1,0:T(8,128)S(1)} copy-done((f32[40,4096]{1,0:T(8,128)S(1)}, f32[40,4096]{1,0:T(8,128)}, u32[]{:S(2)}) %copy-start.1) | copy-done | bytes 655384
  19.7 0.0 copy-start.3
  19.7 0.7 copy-done.3
  20.4 4.7 %dose_products.1.dproj_ref = f32[72,1024]{1,0:T(8,128)S(1)} custom-call(bf16[1024,4096]{1,0:T(8,128)(2,1)} %dose_hbm.3, f32[40,4096]{1,0:T(8,128)S(1)} %copy-done.1, s32[1,4096]{1,0:T(1,128)S(1)} %bitcast.6), custom_call_target="tpu_custom_call" | custom-call | flops 2147483648 | bytes 8388608 | tf_op jit(solution)/shard_map/dose_products/pallas_call | solution.py:178
  25.1 6.8 %all-to-all-done.parts_ref = f32[32,24,128]{2,1,0:T(8,128)S(1)} async-done(((f32[32,24,128]{2,1,0:T(8,128)}), f32[32,24,128]{2,1,0:T(8,128)S(1)}, u32[]{:S(2)}, u32[]{:S(2)}) %all-to-all-start) | async-done | bytes 393248 | tf_op jit(solution)/shard_map/all_to_all | solution.py:500
  31.9 0.4 rank_table.1
  32.3 18.9 %all_to_all.15 = f32[32,24,128]{2,1,0:T(8,128)S(1)} all-to-all(f32[32,24,128]{2,1,0:T(8,128)S(1)} %rank_table.1), channel_id=1, replica_groups=mesh['samp'=32,'prot'=8] {'samp'}, dimensions={0} | all-to-all | bytes 786432 | tf_op jit(solution)/shard_map/all_to_all | solution.py:504
  51.2 0.0 copy-done.2
  51.2 0.0 copy-done
  51.2 0.0 copy-done.4
  51.2 7.2 %cross_products.1 = (f32[448,128]{1,0:T(8,128)S(1)}, f32[448,128]{1,0:T(8,128)S(1)}, f32[448,128]{1,0:T(8,128)S(1)}, f32[448,128]{1,0:T(8,128)S(1)}) custom-call(s32[92,4096]{1,0:T(8,128)S(1)} %copy-done, f32[768,128]{1,0:T(8,128)S(1)} %bitcast.3, bf16[1024,4096]{1,0:T(8,128)(2,1)} %dose_hbm.3, f32[40,4096]{1,0:T(8,128)S(1)} %copy-done.2, ...), custom_call_target="tpu_custom_call" | custom-call | tf_op jit(solution)/shard_map/cross_products/pallas_call | solution.py:366
  58.4 1.2 %collective-permute-start = (f32[448,128]{1,0:T(8,128)S(1)}, f32[448,128]{1,0:T(8,128)S(1)}, u32[]{:S(2)}, u32[]{:S(2)}) collective-permute-start(f32[448,128]{1,0:T(8,128)S(1)} %get-tuple-element.21), channel_id=1, source_target_pairs={{0,64},{8,72},{16,80},{24,88},{32,96},{40,104},{48,112},{56,120},{... | collective-permute-start | bytes 688136 | tf_op jit(solution)/shard_map/ppermute | solution.py:513
  59.6 2.4 %collective-permute-start.1 = (f32[448,128]{1,0:T(8,128)S(1)}, f32[448,128]{1,0:T(8,128)S(1)}, u32[]{:S(2)}, u32[]{:S(2)}) collective-permute-start(f32[448,128]{1,0:T(8,128)S(1)} %get-tuple-element.22), channel_id=1, source_target_pairs={{0,128},{8,136},{16,144},{24,152},{32,160},{40,168},{48,176},{56,1... | collective-permute-start | bytes 688136 | tf_op jit(solution)/shard_map/ppermute | solution.py:513
  61.9 0.8 collective-permute-start.2
  62.7 3.6 %inverse_factor.1.inverse_ref = f32[64,64]{1,0:T(8,128)S(1)} custom-call(f32[768,128]{1,0:T(8,128)S(1)} %bitcast.4), custom_call_target="tpu_custom_call" | custom-call | flops 4000000000 | bytes 32768 | tf_op jit(solution)/shard_map/inverse_factor/pallas_call | solution.py:445
  66.3 0.0 collective-permute-done.first_ref
  66.3 1.1 %collective-permute-done.1.second_ref = f32[448,128]{1,0:T(8,128)S(1)} collective-permute-done((f32[448,128]{1,0:T(8,128)S(1)}, f32[448,128]{1,0:T(8,128)S(1)}, u32[]{:S(2)}, u32[]{:S(2)}) %collective-permute-start.1) | collective-permute-done | bytes 229408 | tf_op jit(solution)/shard_map/ppermute | solution.py:513
  67.5 2.4 %collective-permute-done.2.third_ref = f32[448,128]{1,0:T(8,128)S(1)} collective-permute-done((f32[448,128]{1,0:T(8,128)S(1)}, f32[448,128]{1,0:T(8,128)S(1)}, u32[]{:S(2)}, u32[]{:S(2)}) %collective-permute-start.2) | collective-permute-done | bytes 229408 | tf_op jit(solution)/shard_map/ppermute | solution.py:513
  69.8 0.1 regroup.1
  70.0 19.2 %all_to_all.16.parts_ref = f32[8,96,128]{2,1,0:T(8,128)S(1)} all-to-all(f32[8,96,128]{2,1,0:T(8,128)S(1)} %regroup.1), channel_id=1, replica_groups={{0,8,16,24,32,40,48,56},{64,72,80,88,96,104,112,120},{128,136,144,152,1..., dimensions={0} | all-to-all | bytes 786432 | tf_op jit(solution)/shard_map/all_to_all | solution.py:516
  89.1 1.1 %finish.1 = f32[32,92]{1,0:T(8,128)} custom-call(f32[8,96,128]{2,1,0:T(8,128)S(1)} %all_to_all.16.parts_ref, f32[64,64]{1,0:T(8,128)S(1)} %inverse_factor.1.inverse_ref), custom_call_target="tpu_custom_call" | custom-call | tf_op jit(solution)/shard_map/finish/pallas_call | solution.py:484
Async XLA Ops:
  0.0 51.2 %copy-start.2 = (f32[40,4096]{1,0:T(8,128)S(1)}, f32[40,4096]{1,0:T(8,128)}, u32[]{:S(2)}) copy-start(f32[40,4096]{1,0:T(8,128)} %cov_hbm.3) | copy-start | bytes 1966084
  0.0 51.2 %copy-start = (s32[92,4096]{1,0:T(8,128)S(1)}, s32[92,4096]{1,0:T(8,128)}, u32[]{:S(2)}) copy-start(s32[92,4096]{1,0:T(8,128)} %bins_hbm.3) | copy-start | bytes 4521988
  0.0 51.2 %copy-start.4 = (s32[4096]{0:T(1024)S(1)}, s32[4096]{0:T(1024)}, u32[]{:S(2)}) copy-start(s32[4096]{0:T(1024)} %param.5) | copy-start | bytes 49156
  6.9 25.0 %all-to-all-start = ((f32[32,24,128]{2,1,0:T(8,128)}), f32[32,24,128]{2,1,0:T(8,128)S(1)}, u32[]{:S(2)}, u32[]{:S(2)}) async-start(f32[32,24,128]{2,1,0:T(8,128)} %bitcast.8), calls=%async_computation | async-start | bytes 786432 | tf_op jit(solution)/shard_map/all_to_all | solution.py:500
  18.6 1.1 %copy-start.1 = (f32[40,4096]{1,0:T(8,128)S(1)}, f32[40,4096]{1,0:T(8,128)}, u32[]{:S(2)}) copy-start(f32[40,4096]{1,0:T(8,128)} %cov_hbm.3) | copy-start | bytes 1966084
  19.7 0.7 copy-start.3
  58.4 8.0 %collective-permute-start = (f32[448,128]{1,0:T(8,128)S(1)}, f32[448,128]{1,0:T(8,128)S(1)}, u32[]{:S(2)}, u32[]{:S(2)}) collective-permute-start(f32[448,128]{1,0:T(8,128)S(1)} %get-tuple-element.21), channel_id=1, source_target_pairs={{0,64},{8,72},{16,80},{24,88},{32,96},{40,104},{48,112},{56,120},{... | collective-permute-start | bytes 688136 | tf_op jit(solution)/shard_map/ppermute | solution.py:513
  59.6 7.9 %collective-permute-start.1 = (f32[448,128]{1,0:T(8,128)S(1)}, f32[448,128]{1,0:T(8,128)S(1)}, u32[]{:S(2)}, u32[]{:S(2)}) collective-permute-start(f32[448,128]{1,0:T(8,128)S(1)} %get-tuple-element.22), channel_id=1, source_target_pairs={{0,128},{8,136},{16,144},{24,152},{32,160},{40,168},{48,176},{56,1... | collective-permute-start | bytes 688136 | tf_op jit(solution)/shard_map/ppermute | solution.py:513
  61.9 7.9 %collective-permute-start.2 = (f32[448,128]{1,0:T(8,128)S(1)}, f32[448,128]{1,0:T(8,128)S(1)}, u32[]{:S(2)}, u32[]{:S(2)}) collective-permute-start(f32[448,128]{1,0:T(8,128)S(1)} %get-tuple-element.23), channel_id=1, source_target_pairs={{0,192},{8,200},{16,208},{24,216},{32,224},{40,232},{48,240},{56,2... | collective-permute-start | bytes 688136 | tf_op jit(solution)/shard_map/ppermute | solution.py:513

commit v6 on v5

--- a/solution.py
+++ b/solution.py
@@ -344,17 +344,22 @@
         first = pl.multiple_of(256 * x, 256)
         second = pl.multiple_of(256 * x + LANES, LANES)
         rows = total_ref[pl.ds(first, 256), :]
-        out_ref[0:256, :] = rows[:, :LANES] + rows[:, LANES:]
         low = dproj_ref[:, pl.ds(first, LANES)]
         high = dproj_ref[:, pl.ds(second, LANES)]
-        out_ref[256:320, :] = low[0:64]
-        out_ref[320:384, :] = high[0:64]
+        cross = rows[:, :LANES] + rows[:, LANES:]
+        for n, part in enumerate((low, high)):
+            turned = jnp.concatenate([jnp.zeros((96, LANES), F32), part[0:32]], axis=0).T
+            out_ref[LANES * n : LANES * (n + 1), :] = jnp.where(
+                lane_ids((LANES, LANES)) >= 96, turned, cross[LANES * n : LANES * (n + 1)]
+            )
+        out_ref[256:288, :] = low[32:64]
+        out_ref[288:320, :] = high[32:64]
         dose_own = []
         for z in range(8):
             row = (low, high)[z // 4][64:65]
             dose_own.append(pltpu.roll(row, 96 - 32 * (z % 4), 1) if z % 4 < 3 else row)
         pieces = jnp.concatenate(own + dose_own + [jnp.zeros((53, LANES), F32)], axis=0)
-        out_ref[384:448, :] = jnp.where(spare, pieces, proj)
+        out_ref[320:384, :] = jnp.where(spare, pieces, proj)
 
 
 def cross_products(bin_ids, table, dosages, covariates, plates, dose_proj):
@@ -367,7 +372,7 @@
         cross_kernel,
         in_specs=[hbm, whole, hbm, hbm, hbm, whole],
         out_specs=[whole] * 4,
-        out_shape=[jax.ShapeDtypeStruct((448, LANES), F32)] * 4,
+        out_shape=[jax.ShapeDtypeStruct((384, LANES), F32)] * 4,
         scratch_shapes=[
             pltpu.VMEM((steps, bin_ids.shape[0], chunk), jnp.int32),
             pltpu.VMEM((COVARS, width), F32),
@@ -386,14 +391,21 @@
 
 def regroup_kernel(own_ref, first_ref, second_ref, third_ref, out_ref):
     total = own_ref[...] + first_ref[...] + second_ref[...] + third_ref[...]
-    proj = total[384:448]
+    proj = total[320:384]
+    halves = [
+        jnp.concatenate(
+            [total[LANES * n : LANES * (n + 1)].T[96:128], total[256 + 32 * n : 288 + 32 * n]],
+            axis=0,
+        )
+        for n in range(2)
+    ]
     for z in range(8):
         squares = jnp.concatenate(
             [proj[0:3], proj[3 + z : 4 + z], jnp.zeros((28, LANES), F32)], axis=0
         )
         cross = total[32 * z : 32 * z + 32]
         out_ref[z, 0:32, :] = jnp.where(lane_ids((32, LANES)) >= 96, squares, cross)
-        dose = total[256 + 64 * (z // 4) : 320 + 64 * (z // 4)]
+        dose = halves[z // 4]
         dose = pltpu.roll(dose, 96 - 32 * (z % 4), 1) if z % 4 < 3 else dose
         out_ref[z, 32:96, :] = jnp.where(lane_ids((64, LANES)) >= 96, dose, proj)
 

time: 90.6 us -> 88.9 us (0.981)
  waiting for transfers between devices: 10.3 us -> 9.32 us
    ppermute x3, waiting for transfers between devices: 3.5 us -> 2.5 us  [body(): moved[d] = lax.ppermute(others[d - 1], 'samp', pairs)]
where the time goes in v6:
time: 88.9 us; the launch traced here: 88.6 us
  blocking collectives  37.3 us (42%)
  Pallas kernels  24.2 us (27%)
  starting transfers between devices  15.9 us (18%)
  waiting for transfers between devices  9.32 us (10%)
  local copies, waits for them, and re-layouts  1.81 us (2%)
    all_to_all x1, blocking collectives, body(): table = lax.all_to_all(table, 'samp', 0, 0, tiled=True).reshape(768, LANES)  18.9 us
    all_to_all x1, blocking collectives, body(): lax.all_to_all(parts, 'samp', 0, 0, axis_index_groups=z_groups, tiled=True)  18.4 us
    all_to_all x1, starting transfers between devices, body(): counts = lax.all_to_all(counts, 'samp', 0, 0, tiled=True)  11.6 us
    pallas_call x1, Pallas kernels, cross_products(): pl.pallas_call(cross_kernel, in_specs=[hbm, whole, hbm, hbm, hbm, whole],...  7.23 us
    pallas_call x1, Pallas kernels, histogram(): pl.pallas_call(hist_kernel, in_specs=[hbm, hbm, hbm], out_specs=pl.BlockS...  6.92 us
    all_to_all x1, waiting for transfers between devices, body(): counts = lax.all_to_all(counts, 'samp', 0, 0, tiled=True)  6.82 us
    pallas_call x1, Pallas kernels, dose_products(): pl.pallas_call(dose_kernel, in_specs=[pl.BlockSpec(memory_space=pl.ANY),...  4.7 us
    ppermute x3, starting transfers between devices, body(): moved[d] = lax.ppermute(others[d - 1], 'samp', pairs)  4.3 us
  transfers between devices with their start and end apart: 4, of which 3 were waited for; matrix products, arithmetic and copies ran while one was open for 0% of the time, Pallas kernels for 9%

profile of v6, /device:TPU:26, one launch (start us, length us, event | category | flops | bytes accessed | tf_op | source)
XLA Modules:
  0.0 88.6 jit_solution(11670668435838956187)
XLA Ops:
  0.0 0.0 copy-start.2
  0.0 0.0 copy-start
  0.0 0.0 copy-start.4
  0.0 6.9 %histogram.1 = f32[768,128]{1,0:T(8,128)} custom-call(s32[92,4096]{1,0:T(8,128)} %bins_hbm.3, f32[40,4096]{1,0:T(8,128)} %cov_hbm.3, s32[1,4096]{1,0:T(1,128)} %bitcast.5), custom_call_target="tpu_custom_call" | custom-call | tf_op jit(solution)/shard_map/histogram/pallas_call | solution.py:117
  6.9 11.6 %all-to-all-start = ((f32[32,24,128]{2,1,0:T(8,128)}), f32[32,24,128]{2,1,0:T(8,128)S(1)}, u32[]{:S(2)}, u32[]{:S(2)}) async-start(f32[32,24,128]{2,1,0:T(8,128)} %bitcast.8), calls=%async_computation | async-start | bytes 786432 | tf_op jit(solution)/shard_map/all_to_all | solution.py:512
  18.6 0.0 copy-start.1
  18.6 1.1 %copy-done.1 = f32[40,4096]{1,0:T(8,128)S(1)} copy-done((f32[40,4096]{1,0:T(8,128)S(1)}, f32[40,4096]{1,0:T(8,128)}, u32[]{:S(2)}) %copy-start.1) | copy-done | bytes 655384
  19.7 0.0 copy-start.3
  19.7 0.7 copy-done.3
  20.4 4.7 %dose_products.1.dproj_ref = f32[72,1024]{1,0:T(8,128)S(1)} custom-call(bf16[1024,4096]{1,0:T(8,128)(2,1)} %dose_hbm.3, f32[40,4096]{1,0:T(8,128)S(1)} %copy-done.1, s32[1,4096]{1,0:T(1,128)S(1)} %bitcast.6), custom_call_target="tpu_custom_call" | custom-call | flops 2147483648 | bytes 8388608 | tf_op jit(solution)/shard_map/dose_products/pallas_call | solution.py:178
  25.1 6.8 %all-to-all-done.parts_ref = f32[32,24,128]{2,1,0:T(8,128)S(1)} async-done(((f32[32,24,128]{2,1,0:T(8,128)}), f32[32,24,128]{2,1,0:T(8,128)S(1)}, u32[]{:S(2)}, u32[]{:S(2)}) %all-to-all-start) | async-done | bytes 393248 | tf_op jit(solution)/shard_map/all_to_all | solution.py:512
  31.9 0.4 rank_table.1
  32.3 18.9 %all_to_all.15 = f32[32,24,128]{2,1,0:T(8,128)S(1)} all-to-all(f32[32,24,128]{2,1,0:T(8,128)S(1)} %rank_table.1), channel_id=1, replica_groups=mesh['samp'=32,'prot'=8] {'samp'}, dimensions={0} | all-to-all | bytes 786432 | tf_op jit(solution)/shard_map/all_to_all | solution.py:516
  51.2 0.0 copy-done.2
  51.2 0.0 copy-done
  51.2 0.0 copy-done.4
  51.2 7.2 %cross_products.1 = (f32[384,128]{1,0:T(8,128)S(1)}, f32[384,128]{1,0:T(8,128)S(1)}, f32[384,128]{1,0:T(8,128)S(1)}, f32[384,128]{1,0:T(8,128)S(1)}) custom-call(s32[92,4096]{1,0:T(8,128)S(1)} %copy-done, f32[768,128]{1,0:T(8,128)S(1)} %bitcast.3, bf16[1024,4096]{1,0:T(8,128)(2,1)} %dose_hbm.3, f32[40,4096]{1,0:T(8,128)S(1)} %copy-done.2, ...), custom_call_target="tpu_custom_call" | custom-call | tf_op jit(solution)/shard_map/cross_products/pallas_call | solution.py:371
  58.4 1.2 %collective-permute-start = (f32[384,128]{1,0:T(8,128)S(1)}, f32[384,128]{1,0:T(8,128)S(1)}, u32[]{:S(2)}, u32[]{:S(2)}) collective-permute-start(f32[384,128]{1,0:T(8,128)S(1)} %get-tuple-element.21), channel_id=1, source_target_pairs={{0,64},{8,72},{16,80},{24,88},{32,96},{40,104},{48,112},{56,120},{... | collective-permute-start | bytes 589832 | tf_op jit(solution)/shard_map/ppermute | solution.py:525
  59.6 2.4 %collective-permute-start.1 = (f32[384,128]{1,0:T(8,128)S(1)}, f32[384,128]{1,0:T(8,128)S(1)}, u32[]{:S(2)}, u32[]{:S(2)}) collective-permute-start(f32[384,128]{1,0:T(8,128)S(1)} %get-tuple-element.22), channel_id=1, source_target_pairs={{0,128},{8,136},{16,144},{24,152},{32,160},{40,168},{48,176},{56,1... | collective-permute-start | bytes 589832 | tf_op jit(solution)/shard_map/ppermute | solution.py:525
  61.9 0.8 collective-permute-start.2
  62.7 3.6 %inverse_factor.1.inverse_ref = f32[64,64]{1,0:T(8,128)S(1)} custom-call(f32[768,128]{1,0:T(8,128)S(1)} %bitcast.4), custom_call_target="tpu_custom_call" | custom-call | flops 4000000000 | bytes 32768 | tf_op jit(solution)/shard_map/inverse_factor/pallas_call | solution.py:457
  66.4 0.0 collective-permute-done.first_ref
  66.4 0.5 collective-permute-done.1.second_ref
  66.9 2.0 %collective-permute-done.2.third_ref = f32[384,128]{1,0:T(8,128)S(1)} collective-permute-done((f32[384,128]{1,0:T(8,128)S(1)}, f32[384,128]{1,0:T(8,128)S(1)}, u32[]{:S(2)}, u32[]{:S(2)}) %collective-permute-start.2) | collective-permute-done | bytes 196640 | tf_op jit(solution)/shard_map/ppermute | solution.py:525
  68.9 0.2 regroup.1
  69.1 18.4 %all_to_all.16.parts_ref = f32[8,96,128]{2,1,0:T(8,128)S(1)} all-to-all(f32[8,96,128]{2,1,0:T(8,128)S(1)} %regroup.1), channel_id=1, replica_groups={{0,8,16,24,32,40,48,56},{64,72,80,88,96,104,112,120},{128,136,144,152,1..., dimensions={0} | all-to-all | bytes 786432 | tf_op jit(solution)/shard_map/all_to_all | solution.py:528
  87.5 1.1 %finish.1 = f32[32,92]{1,0:T(8,128)} custom-call(f32[8,96,128]{2,1,0:T(8,128)S(1)} %all_to_all.16.parts_ref, f32[64,64]{1,0:T(8,128)S(1)} %inverse_factor.1.inverse_ref), custom_call_target="tpu_custom_call" | custom-call | tf_op jit(solution)/shard_map/finish/pallas_call | solution.py:496
Async XLA Ops:
  0.0 51.2 %copy-start.2 = (f32[40,4096]{1,0:T(8,128)S(1)}, f32[40,4096]{1,0:T(8,128)}, u32[]{:S(2)}) copy-start(f32[40,4096]{1,0:T(8,128)} %cov_hbm.3) | copy-start | bytes 1966084
  0.0 51.2 %copy-start = (s32[92,4096]{1,0:T(8,128)S(1)}, s32[92,4096]{1,0:T(8,128)}, u32[]{:S(2)}) copy-start(s32[92,4096]{1,0:T(8,128)} %bins_hbm.3) | copy-start | bytes 4521988
  0.0 51.2 %copy-start.4 = (s32[4096]{0:T(1024)S(1)}, s32[4096]{0:T(1024)}, u32[]{:S(2)}) copy-start(s32[4096]{0:T(1024)} %param.5) | copy-start | bytes 49156
  6.9 25.0 %all-to-all-start = ((f32[32,24,128]{2,1,0:T(8,128)}), f32[32,24,128]{2,1,0:T(8,128)S(1)}, u32[]{:S(2)}, u32[]{:S(2)}) async-start(f32[32,24,128]{2,1,0:T(8,128)} %bitcast.8), calls=%async_computation | async-start | bytes 786432 | tf_op jit(solution)/shard_map/all_to_all | solution.py:512
  18.6 1.1 %copy-start.1 = (f32[40,4096]{1,0:T(8,128)S(1)}, f32[40,4096]{1,0:T(8,128)}, u32[]{:S(2)}) copy-start(f32[40,4096]{1,0:T(8,128)} %cov_hbm.3) | copy-start | bytes 1966084
  19.7 0.7 copy-start.3
  58.4 8.0 %collective-permute-start = (f32[384,128]{1,0:T(8,128)S(1)}, f32[384,128]{1,0:T(8,128)S(1)}, u32[]{:S(2)}, u32[]{:S(2)}) collective-permute-start(f32[384,128]{1,0:T(8,128)S(1)} %get-tuple-element.21), channel_id=1, source_target_pairs={{0,64},{8,72},{16,80},{24,88},{32,96},{40,104},{48,112},{56,120},{... | collective-permute-start | bytes 589832 | tf_op jit(solution)/shard_map/ppermute | solution.py:525
  59.6 7.3 %collective-permute-start.1 = (f32[384,128]{1,0:T(8,128)S(1)}, f32[384,128]{1,0:T(8,128)S(1)}, u32[]{:S(2)}, u32[]{:S(2)}) collective-permute-start(f32[384,128]{1,0:T(8,128)S(1)} %get-tuple-element.22), channel_id=1, source_target_pairs={{0,128},{8,136},{16,144},{24,152},{32,160},{40,168},{48,176},{56,1... | collective-permute-start | bytes 589832 | tf_op jit(solution)/shard_map/ppermute | solution.py:525
  61.9 6.9 %collective-permute-start.2 = (f32[384,128]{1,0:T(8,128)S(1)}, f32[384,128]{1,0:T(8,128)S(1)}, u32[]{:S(2)}, u32[]{:S(2)}) collective-permute-start(f32[384,128]{1,0:T(8,128)S(1)} %get-tuple-element.23), channel_id=1, source_target_pairs={{0,192},{8,200},{16,208},{24,216},{32,224},{40,232},{48,240},{56,2... | collective-permute-start | bytes 589832 | tf_op jit(solution)/shard_map/ppermute | solution.py:525
